TPU v7x, 256 devices: a whole 4x4x8 slice. The times are simulated.
256 devices in a mesh: seg: 16 (over z_lo, y), head: 8 (over x, core), rep: 2 (over z_hi).
Axes of the slice: x: 4, y: 4, z: 8 (z_hi: 2, z_lo: 4; z = z_hi * 4 + z_lo), core: 2. Of those that a mesh axis runs over, the one named last changes fastest.
Arguments:
- queries: bfloat16 [4096, 8192], P(('seg', 'rep'), 'head'), may hold values from -4 to 64
- criteria_keys: bfloat16 [4096, 1024], P(('seg', 'rep'), 'head'), may hold values from -8 to 40
- criteria_values: bfloat16 [4096, 1024], P(('seg', 'rep'), 'head'), may hold values from -6 to 6
- candidate_keys: bfloat16 [16384, 1024], P(('seg', 'rep'), 'head'), may hold values from -8 to 8
- candidate_values: bfloat16 [16384, 1024], P(('seg', 'rep'), 'head'), may hold values from -6 to 6
- lengths: int32 [16], replicated, may hold values from 1 to 1024, 10240 in all
- orders: int32 [16, 16], replicated, may hold values from 0 to 15, each once within a row
- out_weight: bfloat16 [8192, 8192], P('rep', 'head'), may hold values from -1 to 1
Outputs:
- projected: bfloat16 [4096, 8192], P(('seg', 'rep'), 'head')
Inputs may be any that keep to these rules, and one draw needn't show every extreme that they name: `lengths`: they sum to 10240, and at least one answer fills all 1024 slots. `orders`: each row is a permutation of the answers.
All inputs are finite; a program needn't handle non-finite values.
Results may differ from a plain program's by a relative error of at most 0.013.
Values may be sent and summed in bfloat16 or wider, within the bound.
A program may use at most 128 MiB of HBM per device.

v0:
```python
import math

import jax
import jax.numpy as jnp
from jax import lax
from jax.sharding import PartitionSpec as P

QUERY_HEADS = 64
KEY_VALUE_HEADS = 8
HEAD_WIDTH = 128
ANSWER_LENGTH = 1024
RUBRIC_LENGTH = 4096


theta_base = 1000000.0
masked_score = -1e30


def apply_rotary(vectors, positions):
    halfway = vectors.shape[-1] // 2
    frequency = jnp.exp(
        jnp.arange(halfway, dtype=jnp.float32) * (-2.0 * math.log(theta_base) / vectors.shape[-1])
    )
    angles = positions.astype(jnp.float32)[:, None] * frequency[None, :]
    cos_table = jnp.cos(angles)[:, None, :]
    sin_table = jnp.sin(angles)[:, None, :]
    front_half = vectors[..., :halfway]
    back_half = vectors[..., halfway:]
    return jnp.concatenate(
        [
            front_half * cos_table - back_half * sin_table,
            back_half * cos_table + front_half * sin_table,
        ],
        axis=-1,
    )


def lookup(small_table, indices):
    matches = indices[:, None] == jnp.arange(small_table.shape[0], dtype=jnp.int32)[None, :]
    return jnp.sum(jnp.where(matches, small_table[None, :], 0), axis=1)


def attend_block(running, rotated_query, key_block, value_block, pos_block, live_block):
    row_peak, row_total, weighted = running
    head_count = rotated_query.shape[0]
    key_rot = apply_rotary(
        key_block.astype(jnp.float32).reshape(key_block.shape[0], head_count, -1), pos_block
    ).astype(jnp.bfloat16)
    value_heads = value_block.reshape(value_block.shape[0], head_count, -1)
    scores = jnp.einsum(
        "hqd,khd->hqk", rotated_query, key_rot, preferred_element_type=jnp.float32
    ) * rotated_query.shape[-1] ** (-0.5)
    masked = jnp.where(live_block[None, None, :], scores, masked_score)
    new_peak = jnp.maximum(row_peak, jnp.max(masked, axis=-1))
    weights = jnp.where(live_block[None, None, :], jnp.exp(scores - new_peak[..., None]), 0.0)
    factor = jnp.exp(row_peak - new_peak)
    row_total = row_total * factor + jnp.sum(weights, axis=-1)
    rounded = weights.astype(jnp.bfloat16)
    weighted = weighted * factor[..., None] + jnp.einsum(
        "hqk,khd->hqd", rounded, value_heads, preferred_element_type=jnp.float32
    )
    return (new_peak, row_total, weighted)


def fold_blocks(running, rotated_query, key_piece, value_piece, key_pos, live_keys):
    row_count = key_piece.shape[0]
    block_rows = math.gcd(row_count, 512)
    steps_total = row_count // block_rows
    key_blocks = key_piece.reshape(steps_total, block_rows, key_piece.shape[1])
    value_blocks = value_piece.reshape(steps_total, block_rows, value_piece.shape[1])
    pos_blocks = key_pos.reshape(steps_total, block_rows)
    live_blocks = live_keys.reshape(steps_total, block_rows)

    def advance(carried, inputs):
        key_block, value_block, pos_block, live_block = inputs
        carried = attend_block(
            carried, rotated_query, key_block, value_block, pos_block, live_block
        )
        return (carried, None)

    running, _ = lax.scan(advance, running, (key_blocks, value_blocks, pos_blocks, live_blocks))
    return running


def local(
    queries,
    criteria_keys,
    criteria_values,
    candidate_keys,
    candidate_values,
    lengths,
    orders,
    out_weight,
):
    slab_rows = queries.shape[0]
    kv_local = candidate_keys.shape[1] // HEAD_WIDTH
    query_group_count = QUERY_HEADS // KEY_VALUE_HEADS
    answer_index = lax.axis_index("seg")
    rep_index = lax.axis_index("rep")
    order_row = lax.dynamic_index_in_dim(orders, answer_index, 0, keepdims=False)
    answers = lengths.shape[0]
    placed = order_row[:, None] == jnp.arange(answers, dtype=jnp.int32)[None, :]
    placed_len = jnp.sum(jnp.where(placed, lengths[None, :], 0), axis=1)
    starts = RUBRIC_LENGTH + jnp.cumsum(placed_len) - placed_len
    offsets = jnp.sum(jnp.where(placed, starts[:, None], 0), axis=0)
    query_pos = (
        RUBRIC_LENGTH
        + jnp.sum(lengths)
        + rep_index * slab_rows
        + jnp.arange(slab_rows, dtype=jnp.int32)
    )
    rotated_query = apply_rotary(
        queries.astype(jnp.float32).reshape(slab_rows, kv_local * query_group_count, HEAD_WIDTH),
        query_pos,
    ).astype(jnp.bfloat16)
    rotated_query = jnp.transpose(
        rotated_query.reshape(slab_rows, kv_local, query_group_count, HEAD_WIDTH), (1, 0, 2, 3)
    ).reshape(kv_local, slab_rows * query_group_count, HEAD_WIDTH)
    running = (
        jnp.full((kv_local, slab_rows * query_group_count), masked_score, jnp.float32),
        jnp.zeros((kv_local, slab_rows * query_group_count), jnp.float32),
        jnp.zeros((kv_local, slab_rows * query_group_count, HEAD_WIDTH), jnp.float32),
    )
    key_piece = lax.all_gather(criteria_keys, ("seg", "rep"), axis=0, tiled=True)
    value_piece = lax.all_gather(criteria_values, ("seg", "rep"), axis=0, tiled=True)
    row_count = key_piece.shape[0]
    key_pos = jnp.arange(row_count, dtype=jnp.int32)
    running = fold_blocks(
        running, rotated_query, key_piece, value_piece, key_pos, jnp.ones((row_count,), dtype=bool)
    )
    key_piece = lax.all_gather(candidate_keys, ("seg", "rep"), axis=0, tiled=True)
    value_piece = lax.all_gather(candidate_values, ("seg", "rep"), axis=0, tiled=True)
    row_count = key_piece.shape[0]
    slot_ids = jnp.arange(row_count, dtype=jnp.int32)
    segment = slot_ids // ANSWER_LENGTH
    within = slot_ids - segment * ANSWER_LENGTH
    key_pos = lookup(offsets, segment) + within
    live_keys = within < lookup(lengths, segment)
    running = fold_blocks(running, rotated_query, key_piece, value_piece, key_pos, live_keys)
    row_peak, row_total, weighted = running
    attended = weighted / row_total[..., None]
    attended = (
        jnp.transpose(
            attended.reshape(kv_local, slab_rows, query_group_count, HEAD_WIDTH), (1, 0, 2, 3)
        )
        .reshape(slab_rows, kv_local * query_group_count * HEAD_WIDTH)
        .astype(jnp.bfloat16)
    )
    features = lax.all_gather(attended, "head", axis=1, tiled=True)
    projected = jnp.dot(
        features,
        lax.all_gather(out_weight, "rep", axis=0, tiled=True),
        preferred_element_type=jnp.float32,
    )
    return projected.astype(jnp.bfloat16)


def solution(mesh):
    placed = (
        P(("seg", "rep"), "head"),
        P(("seg", "rep"), "head"),
        P(("seg", "rep"), "head"),
        P(("seg", "rep"), "head"),
        P(("seg", "rep"), "head"),
        P(),
        P(),
        P("rep", "head"),
    )
    return jax.shard_map(
        local, mesh=mesh, in_specs=placed, out_specs=P(("seg", "rep"), "head"), check_vma=False
    )
```

profile of v0, /device:TPU:42, one launch (start us, length us, event | category | flops | bytes accessed | tf_op | source)
XLA Modules:
  0.0 1479.6 jit_solution(11320587748903204029)
XLA Ops:
  15.7 172.5 %all-gather.7.cloned.1.call-done = bf16[4096,128]{1,0:T(8,128)(2,1)} async-done(((bf16[128,128]{1,0:T(8,128)(2,1)}), bf16[4096,128]{1,0:T(8,128)(2,1)}) %all-gather.7.cloned.1.call-update) | async-done | bytes 1048592 | tf_op jit(solution)/shard_map/all_gather | solution.py:124
  188.2 176.0 %all-gather.9.cloned.1.call-done = bf16[4096,128]{1,0:T(8,128)(2,1)} async-done(((bf16[128,128]{1,0:T(8,128)(2,1)}), bf16[4096,128]{1,0:T(8,128)(2,1)}) %all-gather.9.cloned.1.call-update) | async-done | bytes 1048592 | tf_op jit(solution)/shard_map/all_gather | solution.py:125
  364.2 37.5 %while.30 = (s32[]{:T(128)}, f32[1,1024]{1,0:T(1,128)S(1)}, f32[1,1024]{1,0:T(1,128)S(1)}, f32[1,1024,128]{2,1,0:T(8,128)S(1)}, bf16[8,512,128]{2,1,0:T(8,128)(2...) while((s32[]{:T(128)}, f32[1,1024]{1,0:T(1,128)S(1)}, ...), condition=%wide.region_4.5_spmd.clone, body=%wide.region_1.0_spmd.clone.sunk | while | flops 273651264 | bytes 8723577 | solution.py:81
  401.6 214.7 %all-gather.11.cloned.1.call-done = bf16[16384,128]{1,0:T(8,128)(2,1)} async-done(((bf16[512,128]{1,0:T(8,128)(2,1)}), bf16[16384,128]{1,0:T(8,128)(2,1)}) %all-gather.11.cloned.1.call-update) | async-done | bytes 4194320 | tf_op jit(solution)/shard_map/all_gather | solution.py:131
  616.3 263.6 %all-gather.13.cloned.1.call-done = bf16[16384,128]{1,0:T(8,128)(2,1)} async-done(((bf16[512,128]{1,0:T(8,128)(2,1)}), bf16[16384,128]{1,0:T(8,128)(2,1)}) %all-gather.13.cloned.1.call-update) | async-done | bytes 4194320 | tf_op jit(solution)/shard_map/all_gather | solution.py:132
  879.9 162.2 %while.29 = (s32[]{:T(128)}, f32[1,1024]{1,0:T(1,128)S(1)}, f32[1,1024]{1,0:T(1,128)S(1)}, f32[1,1024,128]{2,1,0:T(8,128)S(1)}, pred[32,512]{1,0:T(8,128)(4,1)S(...) while((s32[]{:T(128)}, f32[1,1024]{1,0:T(1,128)S(1)}, ...), condition=%wide.region_13.14_spmd, body=%wide.region_10.13_spmd.sunk | while | flops 275089984 | bytes 8726129 | solution.py:81
  888.2 1.8 fusion.88
  893.2 1.8 fusion.88
  898.3 1.8 fusion.88
  903.4 1.8 fusion.88
  908.4 1.8 fusion.88
  913.5 1.8 fusion.88
  918.6 1.8 fusion.88
  923.6 1.8 fusion.88
  928.7 1.8 fusion.88
  933.8 1.8 fusion.88
  938.9 1.8 fusion.88
  943.9 1.8 fusion.88
  949.0 1.8 fusion.88
  954.1 1.8 fusion.88
  959.1 1.8 fusion.88
  964.2 1.8 fusion.88
  969.3 1.8 fusion.88
  974.3 1.8 fusion.88
  979.4 1.8 fusion.88
  989.5 1.8 fusion.88
  1004.8 1.8 fusion.88
  1020.0 1.8 fusion.88
  1035.2 1.8 fusion.88
  1043.7 29.6 %all-gather.15.cloned.1.call-done = bf16[128,8192]{1,0:T(8,128)(2,1)} async-done(((bf16[128,1024]{1,0:T(8,128)(2,1)}), bf16[128,8192]{1,0:T(8,128)(2,1)}) %all-gather.15.cloned.1.call-update) | async-done | bytes 2097168 | tf_op jit(solution)/shard_map/all_gather | solution.py:149
  1073.3 390.0 %all-gather.17.cloned.1.call-done = bf16[8192,1024]{1,0:T(8,128)(2,1)} async-done(((bf16[4096,1024]{1,0:T(8,128)(2,1)}), bf16[8192,1024]{1,0:T(8,128)(2,1)}) %all-gather.17.cloned.1.call-update) | async-done | bytes 16777232 | tf_op jit(solution)/shard_map/all_gather | solution.py:152
  1463.3 9.4 convolution_convert_fusion
  (450 shorter events, 164.9 us)
Async XLA Ops:
  6.5 4.2 copy-start
  6.5 181.7 %all-gather.7.cloned.1.call-start = ((), (), s32[]{:S(2)}) async-start(), calls=%async_computation | async-start | bytes 1081344 | tf_op jit(solution)/shard_map/all_gather | solution.py:124
  7.3 356.9 %all-gather.9.cloned.1.call-start = ((), (), s32[]{:S(2)}) async-start(), calls=%async_computation.1 | async-start | bytes 1081344 | tf_op jit(solution)/shard_map/all_gather | solution.py:125
  8.0 608.3 %all-gather.11.cloned.1.call-start = ((), (), s32[]{:S(2)}) async-start(), calls=%async_computation.2 | async-start | bytes 4325376 | tf_op jit(solution)/shard_map/all_gather | solution.py:131
  8.7 871.1 %all-gather.13.cloned.1.call-start = ((), (), s32[]{:S(2)}) async-start(), calls=%async_computation.3 | async-start | bytes 4325376 | tf_op jit(solution)/shard_map/all_gather | solution.py:132
  9.3 1064.0 %all-gather.15.cloned.1.call-start = ((), (), s32[]{:S(2)}) async-start(), calls=%async_computation.4 | async-start | bytes 2359296 | tf_op jit(solution)/shard_map/all_gather | solution.py:149
  1043.1 420.2 %all-gather.17.cloned.1.call-start = ((), (), s32[]{:S(2)}) async-start(), calls=%async_computation.5 | async-start | bytes 25165824 | tf_op jit(solution)/shard_map/all_gather | solution.py:152
Sparse Core Ops, SparseCore 0:
  9.1 178.9 all-gather.6
  190.0 174.1 all-gather.8
  366.0 250.2 all-gather.10
  617.9 261.8 all-gather.12
  1043.3 30.0 all-gather.14
  1075.0 388.2 all-gather.16
where the time goes:
time: 1490 us; the launch traced here: 1480 us
  waiting for transfers between devices  1250 us (84%)
  other arithmetic  111 us (7%)
  matrix products  99.7 us (7%)
    all_gather x1, waiting for transfers between devices, local(): lax.all_gather(out_weight, 'rep', axis=0, tiled=True)  390 us
    all_gather x1, waiting for transfers between devices, local(): lax.all_gather(candidate_values, ('seg', 'rep'), axis=0, tiled=True)  264 us
    all_gather x1, waiting for transfers between devices, local(): lax.all_gather(candidate_keys, ('seg', 'rep'), axis=0, tiled=True)  215 us
    all_gather x1, waiting for transfers between devices, local(): lax.all_gather(criteria_values, ('seg', 'rep'), axis=0, tiled=True)  176 us
    all_gather x1, waiting for transfers between devices, local(): lax.all_gather(criteria_keys, ('seg', 'rep'), axis=0, tiled=True)  173 us
    dot_general x40, matrix products, attend_block(): jnp.einsum('hqk,khd->hqd', rounded, value_heads, preferred_element_type=j...  70.2 us
    concatenate x42, other arithmetic, apply_rotary(): jnp.concatenate([front_half * cos_table - back_half * sin_table, back_hal...  49.4 us
    convert_element_type x40, other arithmetic, attend_block(): key_block.astype(jnp.float32).reshape(key_block.shape[0], head_count, -1)  37.1 us
  transfers between devices with their start and end apart: 6, of which 6 were waited for; matrix products, arithmetic and copies ran while one was open for 3% of the time, Pallas kernels for 0%

commit v1 on v0

v1 whole, which is shorter than its diff:
```python
import functools
import math

import jax
import jax.numpy as jnp
import numpy as np
from jax import lax
from jax.experimental import pallas as pl
from jax.experimental.pallas import tpu as pltpu
from jax.sharding import PartitionSpec as P

QUERY_HEADS = 64
KEY_VALUE_HEADS = 8
HEAD_WIDTH = 128
ANSWER_LENGTH = 1024
RUBRIC_LENGTH = 4096
THETA = 1000000.0
GROUP = 8
ROWS = 128
SLOTS = 512
RUB = 128
SCALE = math.log2(math.e) / math.sqrt(HEAD_WIDTH)
MESH = pl.DeviceIdType.MESH
F32 = jnp.float32
BF16 = jnp.bfloat16


def tables(pos):
    halfway = HEAD_WIDTH // 2
    frequency = jnp.exp(
        jnp.arange(halfway, dtype=F32) * (-2.0 * math.log(THETA) / HEAD_WIDTH)
    )
    frequency = jnp.concatenate([frequency, frequency])
    angles = pos.astype(F32)[:, None] * frequency[None, :]
    sign = jnp.where(jnp.arange(HEAD_WIDTH) < halfway, -1.0, 1.0).astype(F32)
    return jnp.cos(angles), jnp.sin(angles) * sign[None, :]


def slot_tables():
    halfway = HEAD_WIDTH // 2
    frequency = np.exp(np.arange(halfway) * (-2.0 * math.log(THETA) / HEAD_WIDTH))
    angles = np.arange(ANSWER_LENGTH)[:, None] * frequency[None, :]
    cos, sin = np.cos(angles), np.sin(angles)
    return (
        np.concatenate([cos, cos], axis=1).astype(np.float32),
        np.concatenate([-sin, sin], axis=1).astype(np.float32),
    )


def turn(x, cos, sin):
    return x * cos + pltpu.roll(x, HEAD_WIDTH // 2, 1) * sin


def attend_kernel(
    q_ref, rk_ref, rv_ref, ck_ref, cv_ref, cos_ref, sin_ref, len_ref, jcos_ref, jsin_ref,
    att_ref,
    qbuf, rbuf, cbuf, kj, kk, vaug, acc, peak, obuf, lbuf, osend, lsend,
    qs, qr, rs, rr, cs, cr, os, orr, ls, lr,
):
    seg = lax.axis_index("seg")
    rep = lax.axis_index("rep")
    y = lax.rem(seg, 4)
    z = rep * 4 + lax.div(seg, 4)

    def at(yy, zz):
        yy = lax.rem(yy + 8, 4)
        zz = lax.rem(zz + 16, 8)
        return {"seg": lax.rem(zz, 4) * 4 + yy, "rep": lax.div(zz, 4)}

    def zs(d):
        return lax.rem(z + d + 16, 8)

    def ys(d):
        return lax.rem(y + d + 8, 4)

    def copy(src, dst, ssem, rsem, dev):
        return pltpu.make_async_remote_copy(
            src_ref=src, dst_ref=dst, send_sem=ssem, recv_sem=rsem,
            device_id=dev, device_id_type=MESH,
        )

    up, down, north, south, far = at(y, z + 1), at(y, z - 1), at(y + 1, z), at(y - 1, z), at(y + 2, z)
    barrier = pltpu.get_barrier_semaphore()
    for dev in (up, down, north, south, far):
        pl.semaphore_signal(barrier, inc=1, device_id=dev, device_id_type=MESH)
    pl.semaphore_wait(barrier, 5)

    cq, sq = cos_ref[0:128, :], sin_ref[0:128, :]
    rbuf[z, 0] = turn(rk_ref[...].astype(F32), cos_ref[128:256, :], sin_ref[128:256, :]).astype(BF16)
    rbuf[z, 1] = rv_ref[...]
    own_row = lax.broadcasted_iota(jnp.int32, (SLOTS, HEAD_WIDTH), 0) + rep * SLOTS
    own_len = len_ref[pl.ds(lax.div(seg, 4), 1), :]
    cbuf[z, 0] = ck_ref[...]
    cbuf[z, 1] = jnp.where(own_row < own_len, cv_ref[...].astype(F32), 0.0).astype(BF16)

    def ring(buf, ssem, rsem, step):
        a, b = zs(-step), zs(step)
        if step < 3:
            return (
                copy(buf.at[a], buf.at[a], ssem.at[0, step], rsem.at[0, step], up),
                copy(buf.at[b], buf.at[b], ssem.at[1, step], rsem.at[1, step], down),
            )
        return (
            copy(buf.at[a, 0], buf.at[a, 0], ssem.at[0, step], rsem.at[0, step], up),
            copy(buf.at[b, 1], buf.at[b, 1], ssem.at[1, step], rsem.at[1, step], down),
        )

    def start(pair):
        for c in pair:
            c.start()

    def arrived(pair):
        for c in pair:
            c.wait_recv()

    rub = [ring(rbuf, rs, rr, s) for s in range(4)]
    cand = [ring(cbuf, cs, cr, s) for s in range(4)]
    start(rub[0])
    start(cand[0])

    for h in range(GROUP):
        x = q_ref[:, h * 128 : (h + 1) * 128].astype(F32)
        qbuf[y, h * 128 : (h + 1) * 128, :] = turn(x, cq, sq).astype(BF16)
    qdir = (
        copy(qbuf.at[y], qbuf.at[y], qs.at[0], qr.at[0], north),
        copy(qbuf.at[y], qbuf.at[y], qs.at[1], qr.at[1], south),
    )
    start(qdir)
    south_slot, north_slot = ys(-1), ys(1)
    half = GROUP * ROWS // 2
    qfwd = (
        copy(qbuf.at[south_slot, 0:half], qbuf.at[south_slot, 0:half], qs.at[2], qr.at[2], north),
        copy(qbuf.at[north_slot, half:], qbuf.at[north_slot, half:], qs.at[3], qr.at[3], south),
    )

    arrived(rub[0])
    start(rub[1])
    arrived(rub[1])
    start(rub[2])
    arrived(qdir)
    start(qfwd)
    arrived(rub[2])
    start(rub[3])
    arrived(cand[0])
    start(cand[1])
    arrived(rub[3])

    def flash(slot, first):
        def tile(i, carry):
            rows = pl.ds(pl.multiple_of(i * 256, 256), 256)
            s = lax.dot_general(
                qbuf[slot, rows, :], kk[...], (((1,), (1,)), ((), ())), preferred_element_type=F32
            )
            top = jnp.max(s, axis=1, keepdims=True) * SCALE
            if first:
                new = jnp.broadcast_to(top, (256, 128))
            else:
                old = peak[slot, rows, :]
                new = jnp.maximum(old, top)
            p = jnp.exp2(s * SCALE - new[:, 0:1]).astype(BF16)
            o = jnp.dot(p, vaug[...], preferred_element_type=F32)
            if first:
                acc[slot, rows, :] = o
            else:
                f = jnp.exp2(old - new)
                acc[slot, rows, 0:128] = acc[slot, rows, 0:128] * f + o[:, 0:128]
                acc[slot, rows, 128:256] = acc[slot, rows, 128:256] * f + o[:, 128:256]
            peak[slot, rows, :] = new
            return carry

        lax.fori_loop(0, 4, tile, 0)

    for i in range(8):
        vaug[i * 128 : (i + 1) * 128, 0:128] = rbuf[i, 1]
        kk[i * 128 : (i + 1) * 128, :] = rbuf[i, 0]
    vaug[:, 128:256] = jnp.ones((1024, 128), BF16)
    live_key = rbuf[0, 0][0:1, :].astype(F32)

    flash(y, True)
    flash(ys(1), True)
    flash(ys(-1), True)
    arrived(qfwd)
    flash(ys(2), True)

    row = lax.broadcasted_iota(jnp.int32, (SLOTS, HEAD_WIDTH), 0)

    def live(zz):
        length = len_ref[pl.ds(lax.rem(zz, 4), 1), :]
        return row + lax.div(zz, 4) * SLOTS < length

    def prepare(pair):
        for n, zz in enumerate(pair):
            part = slice(n * SLOTS, (n + 1) * SLOTS)
            rows = pl.ds(pl.multiple_of(lax.div(zz, 4) * SLOTS, SLOTS), SLOTS)
            kj[part, :] = turn(cbuf[zz, 0].astype(F32), jcos_ref[rows, :], jsin_ref[rows, :])
            vaug[part, 0:128] = cbuf[zz, 1]
            vaug[part, 128:256] = jnp.where(live(zz), 1.0, 0.0).astype(BF16)

    def rotate(pair, slot):
        for n, zz in enumerate(pair):
            part = slice(n * SLOTS, (n + 1) * SLOTS)
            index = pl.ds(256 + slot * 4 + lax.rem(zz, 4), 1)
            k = turn(kj[part, :], cos_ref[index, :], sin_ref[index, :])
            kk[part, :] = jnp.where(live(zz), k, live_key).astype(BF16)

    def unit(pair, slot):
        rotate(pair, slot)
        flash(slot, False)

    order = (ys(2), ys(1), ys(-1), y)
    for u in range(3):
        pair = ((z, zs(1)), (zs(-1), zs(2)), (zs(-2), zs(3)))[u]
        prepare(pair)
        unit(pair, order[0])
        unit(pair, order[1])
        arrived(cand[u + 1])
        if u < 2:
            start(cand[u + 2])
        unit(pair, order[2])
        unit(pair, order[3])

    pair = (zs(-3), zs(4))
    prepare(pair)
    eye = lax.broadcasted_iota(jnp.int32, (128, 128), 0) == lax.broadcasted_iota(jnp.int32, (128, 128), 1)
    sends = []
    for n, (slot, dev) in enumerate(((ys(2), far), (ys(1), north), (ys(-1), south), (y, None))):
        unit(pair, slot)
        for h in range(GROUP):
            rows = slice(h * 128, (h + 1) * 128)
            total = acc[slot, rows, 128:256]
            mean = acc[slot, rows, 0:128] / total
            stat = peak[slot, rows, :] + jnp.log2(total)
            stat = jnp.sum(jnp.where(eye, stat, 0.0), axis=0, keepdims=True)
            osend[n, rows, :] = mean.astype(BF16)
            lsend[n, h : h + 1, :] = stat
        if dev is not None:
            pair_out = (
                copy(osend.at[n], obuf.at[n], os.at[n], orr.at[n], dev),
                copy(lsend.at[n], lbuf.at[n], ls.at[n], lr.at[n], dev),
            )
            start(pair_out)
            sends.append(pair_out)
    for pair_out in sends:
        arrived(pair_out)

    stats = [lbuf[0], lbuf[1], lbuf[2], lsend[3]]
    top = functools.reduce(jnp.maximum, stats)
    parts = [jnp.exp2(s - top) for s in stats]
    total = parts[0] + parts[1] + parts[2] + parts[3]
    shares = [p / total for p in parts]
    for h in range(GROUP):
        rows = slice(h * 128, (h + 1) * 128)
        out = None
        for n in range(4):
            w = jnp.broadcast_to(shares[n][h : h + 1, :], (128, 128)).T
            src = obuf[n, rows, :] if n < 3 else osend[3, rows, :]
            term = w * src.astype(F32)
            out = term if out is None else out + term
        att_ref[:, rows] = out.astype(BF16)

    for pairs in (rub, cand, (qdir, qfwd), sends):
        for pair in pairs:
            for c in pair:
                c.wait_send()


def project_kernel(
    att_ref, w_hbm, out_ref,
    wbuf, fbuf, part, got,
    wsem, zsend, zrecv, xs, xr, fs, fr, cs, cr, ps, pr,
):
    head = lax.axis_index("head")
    rep = lax.axis_index("rep")
    x = lax.div(head, 2)
    core = lax.rem(head, 2)
    half = lax.div(head, 4)
    mine = half == rep
    u = lax.rem(x - 2 * rep + 8, 4)
    g = lax.rem(head, 4)

    def copy(src, dst, ssem, rsem, dev):
        return pltpu.make_async_remote_copy(
            src_ref=src, dst_ref=dst, send_sem=ssem, recv_sem=rsem,
            device_id=dev, device_id_type=MESH,
        )

    load = [
        pltpu.make_async_copy(w_hbm.at[pl.ds(i * 1024, 1024)], wbuf.at[pl.ds(i * 1024, 1024)], wsem.at[i])
        for i in range(4)
    ]
    for c in load:
        c.start()
    east = {"head": lax.rem(x + 1, 4) * 2 + core}
    west = {"head": lax.rem(x + 3, 4) * 2 + core}
    other = {"head": x * 2 + 1 - core}
    partner = {"rep": 1 - rep}
    barrier = pltpu.get_barrier_semaphore()
    for dev in (east, west, other, partner):
        pl.semaphore_signal(barrier, inc=1, device_id=dev, device_id_type=MESH)
    pl.semaphore_wait(barrier, 4)

    far = 1 - rep
    swap = copy(att_ref, fbuf.at[g, rep], zsend, zrecv, partner)

    @pl.when(jnp.logical_not(mine))
    def _():
        swap.start()

    @pl.when(mine)
    def _():
        fbuf[g, rep] = att_ref[...]

    low, high = core, 2 + core

    def spread(r, n):
        blk0, blk1 = fbuf.at[low, r], fbuf.at[high, r]

        def source(blk):
            copy(blk, blk, xs.at[n, 0], xr.at[n, 0], east).start()
            copy(blk, blk, xs.at[n, 1], xr.at[n, 1], west).start()
            copy(blk, blk, cs.at[n, 0], cr.at[n, 0], other).start()

        @pl.when(u == 0)
        def _():
            source(blk0)

        @pl.when(u == 1)
        def _():
            source(blk1)

    def collect(r, n):
        blk0, blk1 = fbuf.at[low, r], fbuf.at[high, r]
        o0, o1 = fbuf.at[1 - core, r], fbuf.at[3 - core, r]

        def source_end(blk, theirs, from_east, oblk, otheirs):
            if from_east:
                copy(theirs, theirs, xs.at[n, 1], xr.at[n, 1], west).wait_recv()
            else:
                copy(theirs, theirs, xs.at[n, 0], xr.at[n, 0], east).wait_recv()
            c = copy(theirs, theirs, cs.at[n, 1], cr.at[n, 1], other)
            c.start()
            copy(blk, oblk, cs.at[n, 0], cr.at[n, 0], other).wait_recv()
            c.wait_recv()
            copy(blk, blk, xs.at[n, 0], xr.at[n, 0], east).wait_send()
            copy(blk, blk, xs.at[n, 1], xr.at[n, 1], west).wait_send()
            copy(blk, blk, cs.at[n, 0], cr.at[n, 0], other).wait_send()
            c.wait_send()

        @pl.when(u == 0)
        def _():
            source_end(blk0, blk1, True, o0, o1)

        @pl.when(u == 1)
        def _():
            source_end(blk1, blk0, False, o1, o0)

        def sink(near, other_blk, from_west):
            if from_west:
                copy(near, near, xs.at[n, 0], xr.at[n, 0], east).wait_recv()
                f = copy(near, near, fs.at[n], fr.at[n], east)
            else:
                copy(near, near, xs.at[n, 1], xr.at[n, 1], west).wait_recv()
                f = copy(near, near, fs.at[n], fr.at[n], west)
            f.start()
            c0 = copy(near, near, cs.at[n, 0], cr.at[n, 0], other)
            c0.start()
            copy(other_blk, other_blk, fs.at[n], fr.at[n], other).wait_recv()
            c1 = copy(other_blk, other_blk, cs.at[n, 1], cr.at[n, 1], other)
            c1.start()
            c0.wait_recv()
            c1.wait_recv()
            f.wait_send()
            c0.wait_send()
            c1.wait_send()

        @pl.when(u == 2)
        def _():
            sink(blk1, blk0, True)

        @pl.when(u == 3)
        def _():
            sink(blk0, blk1, False)

    spread(rep, 0)

    @pl.when(mine)
    def _():
        copy(att_ref, fbuf.at[g, far], zsend, zrecv, partner).wait_recv()

    spread(far, 1)
    collect(rep, 0)
    collect(far, 1)
    for c in load:
        c.wait()

    def product(r, columns):
        total = None
        for k in range(4):
            term = jnp.dot(
                fbuf[k, r], wbuf[k * 1024 : (k + 1) * 1024, columns], preferred_element_type=F32
            )
            total = term if total is None else total + term
        return total

    sends = []
    for j in range(4):
        columns = slice(j * 256, (j + 1) * 256)
        part[j] = product(far, columns).astype(BF16)
        c = copy(part.at[j], got.at[j], ps.at[j], pr.at[j], partner)
        c.start()
        sends.append(c)
    for j in range(4):
        columns = slice(j * 256, (j + 1) * 256)
        mine_part = product(rep, columns)
        sends[j].wait_recv()
        out_ref[:, columns] = (mine_part + got[j].astype(F32)).astype(BF16)
    for c in sends:
        c.wait_send()

    @pl.when(jnp.logical_not(mine))
    def _():
        swap.wait_send()


VMEM = pl.BlockSpec(memory_space=pltpu.VMEM)
DMA = pltpu.SemaphoreType.DMA


def local(
    queries, criteria_keys, criteria_values, candidate_keys, candidate_values,
    lengths, orders, out_weight,
):
    seg = lax.axis_index("seg")
    rep = lax.axis_index("rep")
    y, zl = lax.rem(seg, 4), lax.div(seg, 4)
    ids = jnp.arange(16, dtype=jnp.int32)
    views = lax.dynamic_slice_in_dim(orders, zl * 4, 4, 0)
    placed = views[:, :, None] == ids[None, None, :]
    placed_len = jnp.sum(jnp.where(placed, lengths[None, None, :], 0), axis=2)
    before = ids[None, :] < ids[:, None]
    starts = RUBRIC_LENGTH + jnp.sum(jnp.where(before[None], placed_len[:, None, :], 0), axis=2)
    offsets = jnp.sum(jnp.where(placed, starts[:, :, None], 0), axis=1)
    wanted = jnp.arange(4, dtype=jnp.int32) * 4 + y
    pick = wanted[:, None] == ids[None, :]
    offsets = jnp.sum(jnp.where(pick[None], offsets[:, None, :], 0), axis=2)
    mine = jnp.sum(jnp.where(pick, lengths[None, :], 0), axis=1)
    mine = jnp.broadcast_to(mine[:, None], (4, 128))
    rows = jnp.arange(ROWS, dtype=jnp.int32)
    query_pos = RUBRIC_LENGTH + jnp.sum(lengths) + rep * ROWS + rows
    rubric_pos = (seg * 2 + rep) * RUB + rows
    cos, sin = tables(jnp.concatenate([query_pos, rubric_pos, offsets.reshape(16)]))
    jcos, jsin = slot_tables()

    attended = pl.pallas_call(
        attend_kernel,
        out_shape=jax.ShapeDtypeStruct((ROWS, 1024), BF16),
        in_specs=[VMEM] * 10,
        out_specs=VMEM,
        scratch_shapes=[
            pltpu.VMEM((4, 1024, 128), BF16),
            pltpu.VMEM((8, 2, RUB, 128), BF16),
            pltpu.VMEM((8, 2, SLOTS, 128), BF16),
            pltpu.VMEM((1024, 128), F32),
            pltpu.VMEM((1024, 128), BF16),
            pltpu.VMEM((1024, 256), BF16),
            pltpu.VMEM((4, 1024, 256), F32),
            pltpu.VMEM((4, 1024, 128), F32),
            pltpu.VMEM((3, 1024, 128), BF16),
            pltpu.VMEM((3, 8, 128), F32),
            pltpu.VMEM((4, 1024, 128), BF16),
            pltpu.VMEM((4, 8, 128), F32),
            DMA((4,)), DMA((4,)),
            DMA((2, 4)), DMA((2, 4)),
            DMA((2, 4)), DMA((2, 4)),
            DMA((3,)), DMA((3,)),
            DMA((3,)), DMA((3,)),
        ],
        compiler_params=pltpu.CompilerParams(
            collective_id=0, has_side_effects=True, vmem_limit_bytes=48 * 1024 * 1024
        ),
        name="attend",
    )(
        queries, criteria_keys, criteria_values, candidate_keys, candidate_values,
        cos, sin, mine, jnp.asarray(jcos), jnp.asarray(jsin),
    )
    return pl.pallas_call(
        project_kernel,
        out_shape=jax.ShapeDtypeStruct((ROWS, 1024), BF16),
        in_specs=[VMEM, pl.BlockSpec(memory_space=pl.ANY)],
        out_specs=VMEM,
        scratch_shapes=[
            pltpu.VMEM((4096, 1024), BF16),
            pltpu.VMEM((4, 2, ROWS, 1024), BF16),
            pltpu.VMEM((4, ROWS, 256), BF16),
            pltpu.VMEM((4, ROWS, 256), BF16),
            DMA((4,)),
            DMA, DMA,
            DMA((2, 2)), DMA((2, 2)),
            DMA((2,)), DMA((2,)),
            DMA((2, 2)), DMA((2, 2)),
            DMA((4,)), DMA((4,)),
        ],
        compiler_params=pltpu.CompilerParams(
            collective_id=1, has_side_effects=True, vmem_limit_bytes=48 * 1024 * 1024
        ),
        name="project",
    )(attended, out_weight)


def solution(mesh):
    rows = P(("seg", "rep"), "head")
    return jax.shard_map(
        local,
        mesh=mesh,
        in_specs=(rows, rows, rows, rows, rows, P(), P(), P("rep", "head")),
        out_specs=rows,
        check_vma=False,
    )
```

time: 1490 us -> 166 us (0.11)
  waiting for transfers between devices: 1250 us -> 0 us
  Pallas kernels: 0 us -> 154 us
  other arithmetic: 111 us -> 4.18 us
  matrix products: 99.7 us -> 0 us
    all_gather x6 -> x0, waiting for transfers between devices: 1250 us -> none  [the longest x1 390 us: local(): lax.all_gather(out_weight, 'rep', axis=0, tiled=True)]
    pallas_call x0 -> x2, Pallas kernels: none -> 154 us  [the longest x1 108 us: local(): pl.pallas_call(attend_kernel, out_shape=jax.ShapeDtypeStruct((ROWS, 1024)...]
    dot_general x81 -> x0, matrix products: 99.7 us -> none  [the longest x40 70.2 us: attend_block(): jnp.einsum('hqk,khd->hqd', rounded, value_heads, preferred_element_type=j...]
    concatenate x42 -> x0, other arithmetic: 49.4 us -> none  [apply_rotary(): jnp.concatenate([front_half * cos_table - back_half * sin_table, back_hal...]
    convert_element_type x82 -> x1, other arithmetic: 37.8 us -> 0.01 us  [tables(): angles = pos.astype(F32)[:, None] * frequency[None, :]]
    reduce_sum x44 -> x6, other arithmetic: 20.4 us -> 3.41 us  [the longest x1 1.3 us: local(): query_pos = RUBRIC_LENGTH + jnp.sum(lengths) + rep * ROWS + rows]
  transfers between devices with their start and end apart: 6 -> 0, of which waited for: 6 -> 0; matrix products, arithmetic and copies ran while one was open for 3% -> 0% of each run, Pallas kernels for 0% -> 0%
where the time goes in v1:
time: 166 us
  Pallas kernels  154 us (93%)
  local copies, waits for them, and re-layouts  7.22 us (4%)
  other arithmetic  4.18 us (3%)
    pallas_call x1, Pallas kernels, local(): pl.pallas_call(attend_kernel, out_shape=jax.ShapeDtypeStruct((ROWS, 1024)...  108 us
    pallas_call x1, Pallas kernels, local(): pl.pallas_call(project_kernel, out_shape=jax.ShapeDtypeStruct((ROWS, 1024...  46.2 us
    unnamed x17, local copies, waits for them, and re-layouts  7.06 us

profile of v1, /device:TPU:42, one launch (start us, length us, event | category | flops | bytes accessed | tf_op | source)
XLA Modules:
  0.0 165.9 jit_solution(14632151967166685399)
XLA Ops:
  0.0 0.0 copy-start
  0.0 1.3 reduce_sum.54
  2.0 0.8 select_reduce_fusion.4
  2.8 0.1 iota_compare_fusion.2
  2.9 0.1 compare_select_fusion
  3.0 0.0 copy-done
  3.0 0.1 broadcast_in_dim.114.len_ref
  3.1 0.9 select_reduce_fusion.2
  4.0 0.1 select_reduce_fusion.1
  4.1 0.1 select_reduce_fusion
  4.2 0.2 select_reduce_fusion.3
  4.4 0.1 concatenate.12
  4.5 0.6 fusion
  5.1 0.0 copy-start.1
  5.1 1.0 copy-done.1
  6.1 0.0 copy-start.2
  6.1 1.0 copy-done.2
  7.1 0.0 copy-start.3
  7.1 0.9 copy-done.3
  8.1 0.0 copy-start.4
  8.1 0.9 copy-done.4
  9.0 0.0 copy-start.5
  9.0 0.9 copy-done.5
  9.9 0.0 copy-start.6
  9.9 0.8 copy-done.6
  10.7 0.0 copy-start.7
  10.7 0.8 copy-done.7
  11.4 107.6 %attend.1.att_ref = bf16[128,1024]{1,0:T(8,128)(2,1)S(1)} custom-call(bf16[128,1024]{1,0:T(8,128)(2,1)S(1)} %copy-done.3, bf16[128,128]{1,0:T(8,128)(2,1)S(1)} %copy-done.6, bf16[128,128]{1,0:T(8,128)(2,1)S(1)} %copy-done.7, bf16[512,128]{1,0:T(8,128)(2,1)S(1)} %copy-done.4, bf16[512,128]{1,0:T(8,128)(2,1)S(1)} %copy-done.5, ...), custom_call_target="tpu_custom_call" | custom-call | tf_op jit(solution)/shard_map/attend/pallas_call | solution.py:454
  119.0 46.2 %project.1 = bf16[128,1024]{1,0:T(8,128)(2,1)S(1)} custom-call(bf16[128,1024]{1,0:T(8,128)(2,1)S(1)} %attend.1.att_ref, bf16[4096,1024]{1,0:T(8,128)(2,1)} %w_hbm.1), custom_call_target="tpu_custom_call" | custom-call | tf_op jit(solution)/shard_map/project/pallas_call | solution.py:486
  165.2 0.7 copy.12
  (7 shorter events, 0.1 us)
Async XLA Ops:
  0.0 3.0 %copy-start = (s32[16,16]{1,0:T(8,128)S(1)}, s32[16,16]{1,0:T(8,128)}, u32[]{:S(2)}) copy-start(s32[16,16]{1,0:T(8,128)} %param.16) | copy-start | bytes 3076
  5.1 1.0 copy-start.1
  6.1 1.0 copy-start.2
  7.1 0.9 copy-start.3
  8.1 0.9 copy-start.4
  9.0 0.9 copy-start.5
  9.9 0.8 copy-start.6
  10.7 0.8 copy-start.7

commit v2 on v1

v2 whole, which is shorter than its diff:
```python
import functools
import math

import jax
import jax.numpy as jnp
import numpy as np
from jax import lax
from jax.experimental import pallas as pl
from jax.experimental.pallas import tpu as pltpu
from jax.sharding import PartitionSpec as P

QUERY_HEADS = 64
KEY_VALUE_HEADS = 8
HEAD_WIDTH = 128
ANSWER_LENGTH = 1024
RUBRIC_LENGTH = 4096
THETA = 1000000.0
GROUP = 8
ROWS = 128
SLOTS = 512
RUB = 128
CHUNK = 64
SCALE = math.log2(math.e) / math.sqrt(HEAD_WIDTH)
MESH = pl.DeviceIdType.MESH
F32 = jnp.float32
BF16 = jnp.bfloat16


def tables(pos):
    halfway = HEAD_WIDTH // 2
    frequency = jnp.exp(
        jnp.arange(halfway, dtype=F32) * (-2.0 * math.log(THETA) / HEAD_WIDTH)
    )
    frequency = jnp.concatenate([frequency, frequency])
    angles = pos.astype(F32)[:, None] * frequency[None, :]
    sign = jnp.where(jnp.arange(HEAD_WIDTH) < halfway, -1.0, 1.0).astype(F32)
    return jnp.cos(angles), jnp.sin(angles) * sign[None, :]


def slot_tables():
    halfway = HEAD_WIDTH // 2
    frequency = np.exp(np.arange(halfway) * (-2.0 * math.log(THETA) / HEAD_WIDTH))
    angles = np.arange(ANSWER_LENGTH)[:, None] * frequency[None, :]
    cos, sin = np.cos(angles), np.sin(angles)
    return (
        np.concatenate([cos, cos], axis=1).astype(np.float32),
        np.concatenate([-sin, sin], axis=1).astype(np.float32),
    )


def turn(x, cos, sin):
    return x * cos + pltpu.roll(x, HEAD_WIDTH // 2, 1) * sin


def fused_kernel(
    q_ref, rk_ref, rv_ref, ck_ref, cv_ref, cos_ref, sin_ref, len_ref, jcos_ref, jsin_ref, w_ref,
    out_ref,
    qin, rkin, cvin, cost, sint, lens, jcos, jsin, ocos, osin,
    qbuf, rbuf, cbuf, kjt, kkt, vaug, live_col, acc, peak, obuf, lbuf, osend, lsend,
    wbuf, fbuf, att, part, got,
    ins, ws, qs, qr, rs, rr, cs, cr, os, orr, ls, lr,
    zsend, zrecv, xs, xr, fs, fr, ds, dr, ps, pr,
):
    seg = lax.axis_index("seg")
    rep = lax.axis_index("rep")
    head = lax.axis_index("head")
    y = lax.rem(seg, 4)
    z = rep * 4 + lax.div(seg, 4)
    x = lax.div(head, 2)
    core = lax.rem(head, 2)

    def at(yy, zz):
        yy = lax.rem(yy + 8, 4)
        zz = lax.rem(zz + 16, 8)
        return {"seg": lax.rem(zz, 4) * 4 + yy, "rep": lax.div(zz, 4)}

    def zs(d):
        return lax.rem(z + d + 16, 8)

    def ys(d):
        return lax.rem(y + d + 8, 4)

    def copy(src, dst, ssem, rsem, dev):
        return pltpu.make_async_remote_copy(
            src_ref=src, dst_ref=dst, send_sem=ssem, recv_sem=rsem,
            device_id=dev, device_id_type=MESH,
        )

    def start(pair):
        for c in pair:
            c.start()

    def arrived(pair):
        for c in pair:
            c.wait_recv()

    load = [
        pltpu.make_async_copy(a, b, ins.at[i])
        for i, (a, b) in enumerate((
            (rk_ref, rkin), (rv_ref, rbuf.at[z, 1]), (cos_ref, cost), (sin_ref, sint),
            (cv_ref, cvin), (ck_ref, cbuf.at[z, 0]), (len_ref, lens), (q_ref, qin),
            (jcos_ref, jcos), (jsin_ref, jsin),
        ))
    ]
    start(load)

    up, down = at(y, z + 1), at(y, z - 1)
    north, south, beyond = at(y + 1, z), at(y - 1, z), at(y + 2, z)
    east = {"head": lax.rem(x + 1, 4) * 2 + core}
    west = {"head": lax.rem(x + 3, 4) * 2 + core}
    other = {"head": x * 2 + 1 - core}
    partner = {"rep": 1 - rep}
    barrier = pltpu.get_barrier_semaphore()
    peers = (up, down, north, south, beyond, east, west, other, partner)
    for dev in peers:
        pl.semaphore_signal(barrier, inc=1, device_id=dev, device_id_type=MESH)
    pl.semaphore_wait(barrier, len(peers))

    def ring(buf, ssem, rsem, step):
        a, b = zs(-step), zs(step)
        if step < 3:
            return (
                copy(buf.at[a], buf.at[a], ssem.at[0, step], rsem.at[0, step], up),
                copy(buf.at[b], buf.at[b], ssem.at[1, step], rsem.at[1, step], down),
            )
        return (
            copy(buf.at[a, 0], buf.at[a, 0], ssem.at[0, step], rsem.at[0, step], up),
            copy(buf.at[b, 1], buf.at[b, 1], ssem.at[1, step], rsem.at[1, step], down),
        )

    rub = [ring(rbuf, rs, rr, s) for s in range(4)]
    cand = [ring(cbuf, cs, cr, s) for s in range(4)]
    for c in load[:4]:
        c.wait()
    rbuf[z, 0] = turn(rkin[...].astype(F32), cost[128:256, :], sint[128:256, :]).astype(BF16)
    start(rub[0])
    for c in load[4:7]:
        c.wait()
    own_row = lax.broadcasted_iota(jnp.int32, (SLOTS, HEAD_WIDTH), 0) + rep * SLOTS
    own_len = lens[pl.ds(lax.div(seg, 4), 1), :]
    cbuf[z, 1] = jnp.where(own_row < own_len, cvin[...].astype(F32), 0.0).astype(BF16)
    start(cand[0])
    load[7].wait()
    cq, sq = cost[0:128, :], sint[0:128, :]
    for h in range(GROUP):
        v = qin[:, h * 128 : (h + 1) * 128].astype(F32)
        qbuf[y, h * 128 : (h + 1) * 128, :] = turn(v, cq, sq).astype(BF16)
    qdir = (
        copy(qbuf.at[y], qbuf.at[y], qs.at[0], qr.at[0], north),
        copy(qbuf.at[y], qbuf.at[y], qs.at[1], qr.at[1], south),
    )
    start(qdir)
    south_slot, north_slot = ys(-1), ys(1)
    mid = GROUP * ROWS // 2
    qfwd = (
        copy(qbuf.at[south_slot, 0:mid], qbuf.at[south_slot, 0:mid], qs.at[2], qr.at[2], north),
        copy(qbuf.at[north_slot, mid:], qbuf.at[north_slot, mid:], qs.at[3], qr.at[3], south),
    )
    wload = [
        pltpu.make_async_copy(w_ref.at[pl.ds(i * 1024, 1024)], wbuf.at[pl.ds(i * 1024, 1024)], ws.at[i])
        for i in range(4)
    ]
    start(wload)

    arrived(rub[0])
    start(rub[1])
    for i in range(16):
        ocos[i] = jnp.broadcast_to(cost[256 + i : 257 + i, :], (128, 128)).T
        osin[i] = jnp.broadcast_to(sint[256 + i : 257 + i, :], (128, 128)).T
    arrived(rub[1])
    start(rub[2])
    arrived(qdir)
    start(qfwd)
    load[8].wait()
    load[9].wait()
    arrived(rub[2])
    start(rub[3])
    arrived(cand[0])
    start(cand[1])

    lane = lax.broadcasted_iota(jnp.int32, (1, 128), 1)
    row = lax.broadcasted_iota(jnp.int32, (SLOTS, HEAD_WIDTH), 0)

    def prepare(shards, base):
        for n, zz in enumerate(shards):
            part_rows = slice(base + n * SLOTS, base + (n + 1) * SLOTS)
            place = lax.div(zz, 4) * SLOTS
            rows = pl.ds(pl.multiple_of(place, SLOTS), SLOTS)
            kjt[:, part_rows] = turn(cbuf[zz, 0].astype(F32), jcos[rows, :], jsin[rows, :]).T
            vaug[part_rows, 0:128] = cbuf[zz, 1]
            alive = row + place < lens[pl.ds(lax.rem(zz, 4), 1), :]
            vaug[part_rows, 128:256] = jnp.where(alive, 1.0, 0.0).astype(BF16)

    def rotate(shards, base, slot):
        for n, zz in enumerate(shards):
            length = lens[pl.ds(lax.rem(zz, 4), 1), :]
            place = lax.div(zz, 4) * SLOTS
            co, so = ocos[slot * 4 + lax.rem(zz, 4)], osin[slot * 4 + lax.rem(zz, 4)]
            for i in range(SLOTS // 128):
                cols = slice(base + n * SLOTS + i * 128, base + n * SLOTS + (i + 1) * 128)
                k = kjt[:, cols]
                k = k * co + jnp.concatenate([k[64:], k[:64]], axis=0) * so
                alive = lane + (place + i * 128) < length
                kkt[:, cols] = jnp.where(alive, k, live_col[...]).astype(BF16)

    def flash(slot, keys, first):
        scores = [
            jnp.dot(qbuf[slot, i * 256 : (i + 1) * 256, :], kkt[:, 0:keys], preferred_element_type=F32)
            for i in range(4)
        ]
        for i in range(4):
            rows = slice(i * 256, (i + 1) * 256)
            s = scores[i]
            top = jnp.max(s, axis=1, keepdims=True) * SCALE
            if first:
                new = jnp.broadcast_to(top, (256, 128))
            else:
                old = peak[slot, rows, :]
                new = jnp.maximum(old, top)
            p = jnp.exp2(s * SCALE - new[:, 0:1]).astype(BF16)
            o = jnp.dot(p, vaug[0:keys, :], preferred_element_type=F32)
            if first:
                acc[slot, rows, :] = o
            else:
                f = jnp.exp2(old - new)
                acc[slot, rows, 0:128] = acc[slot, rows, 0:128] * f + o[:, 0:128]
                acc[slot, rows, 128:256] = acc[slot, rows, 128:256] * f + o[:, 128:256]
            peak[slot, rows, :] = new

    shards = (z, zs(1))
    prepare(shards, 1024)
    arrived(rub[3])
    for i in range(8):
        vaug[i * 128 : (i + 1) * 128, 0:128] = rbuf[i, 1]
        kkt[:, i * 128 : (i + 1) * 128] = rbuf[i, 0].astype(F32).T.astype(BF16)
    vaug[0:1024, 128:256] = jnp.ones((1024, 128), BF16)
    live_col[...] = jnp.broadcast_to(rbuf[0, 0][0:1, :].astype(F32), (128, 128)).T

    def unit0(n, carry):
        slot = lax.rem(y + 3 * n, 4)

        @pl.when(n == 2)
        def _():
            arrived(qfwd)
            arrived(cand[1])
            start(cand[2])

        rotate(shards, 1024, slot)
        flash(slot, 2048, True)
        return carry

    lax.fori_loop(0, 4, unit0, 0)

    arrived(cand[2])
    start(cand[3])
    shards1 = (zs(-1), zs(2), zs(-2), zs(3))
    prepare(shards1, 0)

    def unit1(n, carry):
        slot = lax.rem(y + 2 + 3 * n, 4)
        rotate(shards1, 0, slot)
        flash(slot, 2048, False)
        return carry

    lax.fori_loop(0, 4, unit1, 0)

    arrived(cand[3])
    shards2 = (zs(-3), zs(4))
    prepare(shards2, 0)
    eye = lax.broadcasted_iota(jnp.int32, (128, 128), 0) == lax.broadcasted_iota(jnp.int32, (128, 128), 1)

    def outgoing(n, dev):
        return (
            copy(osend.at[n], obuf.at[n], os.at[n], orr.at[n], dev),
            copy(lsend.at[n], lbuf.at[n], ls.at[n], lr.at[n], dev),
        )

    def unit2(n, carry):
        slot = lax.rem(y + 2 + 3 * n, 4)
        rotate(shards2, 0, slot)
        flash(slot, 1024, False)
        for h in range(GROUP):
            rows = slice(h * 128, (h + 1) * 128)
            total = acc[slot, rows, 128:256]
            stat = peak[slot, rows, :] + jnp.log2(total)
            osend[n, rows, :] = (acc[slot, rows, 0:128] / total).astype(BF16)
            lsend[n, h : h + 1, :] = jnp.sum(jnp.where(eye, stat, 0.0), axis=0, keepdims=True)

        @pl.when(n != 2)
        def _():
            start(outgoing(n, at(slot, z)))

        return carry

    lax.fori_loop(0, 4, unit2, 0)
    partials = [outgoing(0, beyond), outgoing(1, north), outgoing(3, south)]
    for pair in partials:
        arrived(pair)

    half = lax.div(head, 4)
    mine = half == rep
    u = lax.rem(x - 2 * rep + 8, 4)
    g = lax.rem(head, 4)
    far = 1 - rep

    stats = [lbuf[0], lbuf[1], lsend[2], lbuf[3]]
    top = functools.reduce(jnp.maximum, stats)
    parts = [jnp.exp2(s - top) for s in stats]
    total = parts[0] + parts[1] + parts[2] + parts[3]
    shares = [p / total for p in parts]
    for h in range(GROUP):
        rows = slice(h * 128, (h + 1) * 128)
        out = None
        for n in range(4):
            w = jnp.broadcast_to(shares[n][h : h + 1, :], (128, 128)).T
            src = osend[2, rows, :] if n == 2 else obuf[n, rows, :]
            term = w * src.astype(F32)
            out = term if out is None else out + term
        att[:, rows] = out.astype(BF16)

    @pl.when(mine)
    def _():
        fbuf[g, rep] = att[...]

    def chunk(i):
        return pl.ds(i * CHUNK, CHUNK)

    swaps = [
        copy(att.at[chunk(i)], fbuf.at[g, rep, chunk(i)], zsend.at[i], zrecv.at[i], partner)
        for i in range(2)
    ]
    swapped = [
        copy(fbuf.at[g, far, chunk(i)], fbuf.at[g, far, chunk(i)], zsend.at[i], zrecv.at[i], partner)
        for i in range(2)
    ]
    items = [(rep, pl.ds(0, ROWS)), (far, chunk(0)), (far, chunk(1))]

    def block(k, n):
        r, rows = items[n]
        return fbuf.at[k, r, rows]

    def hop(blk, n, way):
        return copy(blk, blk, xs.at[n, way], xr.at[n, way], (east, west)[way])

    def cross(blk, n, way):
        return copy(blk, blk, ds.at[n, way], dr.at[n, way], other)

    def source(k, k_other, way_in):
        def send(n):
            start((hop(block(k, n), n, 0), hop(block(k, n), n, 1), cross(block(k, n), n, 0)))

        send(0)
        for i in range(2):
            swapped[i].wait_recv()
            send(i + 1)
        for n in range(3):
            hop(block(k_other, n), n, way_in).wait_recv()
            cross(block(k_other, n), n, 1).start()

    def source_end(n, k, k_other):
        cross(block(k, n), n, 0).wait_recv()
        cross(block(k_other, n), n, 1).wait_recv()

    def sink(k_near, k_far, way):
        start(swaps)
        for n in range(3):
            near = block(k_near, n)
            hop(near, n, way).wait_recv()
            start((copy(near, near, fs.at[n], fr.at[n], (east, west)[way]), cross(near, n, 0)))
            if n:
                pass_on(k_near, k_far, way, n - 1)
        pass_on(k_near, k_far, way, 2)

    def pass_on(k_near, k_far, way, n):
        blk = block(k_far, n)
        copy(blk, blk, fs.at[n], fr.at[n], (east, west)[way]).wait_recv()
        cross(blk, n, 1).start()

    low, high = core, 2 + core
    roles = ((0, low, high), (1, high, low), (2, high, low), (3, low, high))
    for which, k0, k1 in roles:

        @pl.when(u == which)
        def _():
            if which < 2:
                source(k0, k1, 1 - which)
            else:
                sink(k0, k1, which - 2)

    for c in wload:
        c.wait()

    def crossed(n):
        r, rows = items[n]
        blk = fbuf.at[g, r, rows]
        cross(blk, n, 0).wait_recv()
        cross(blk, n, 1).wait_recv()

    def product(r, rows):
        total = None
        for k in range(4):
            term = jnp.dot(
                fbuf[k, r, rows, :], wbuf[k * 1024 : (k + 1) * 1024, :], preferred_element_type=F32
            )
            total = term if total is None else total + term
        return total

    sends = []
    for i in range(2):
        rows = slice(i * CHUNK, (i + 1) * CHUNK)
        crossed(i + 1)
        part[rows, :] = product(far, rows).astype(BF16)
        c = copy(part.at[chunk(i)], got.at[chunk(i)], ps.at[i], pr.at[i], partner)
        c.start()
        sends.append(c)
    crossed(0)
    own = product(rep, slice(0, ROWS))
    for i in range(2):
        rows = slice(i * CHUNK, (i + 1) * CHUNK)
        sends[i].wait_recv()
        out_ref[rows, :] = (own[rows, :] + got[rows, :].astype(F32)).astype(BF16)

    for pairs in (rub, cand, (qdir, qfwd), partials, (sends,)):
        for pair in pairs:
            for c in pair:
                c.wait_send()
    for n in range(3):
        blk = block(g, n)
        cross(blk, n, 0).wait_send()
        cross(blk, n, 1).wait_send()

    @pl.when(mine)
    def _():
        for n in range(3):
            hop(block(g, n), n, 0).wait_send()
            hop(block(g, n), n, 1).wait_send()

    @pl.when(jnp.logical_not(mine))
    def _():
        for n in range(3):
            blk = block(g, n)
            copy(blk, blk, fs.at[n], fr.at[n], east).wait_send()
        for c in swaps:
            c.wait_send()


VMEM = pl.BlockSpec(memory_space=pltpu.VMEM)
ANY = pl.BlockSpec(memory_space=pl.ANY)
DMA = pltpu.SemaphoreType.DMA


def local(
    queries, criteria_keys, criteria_values, candidate_keys, candidate_values,
    lengths, orders, out_weight,
):
    seg = lax.axis_index("seg")
    rep = lax.axis_index("rep")
    y, zl = lax.rem(seg, 4), lax.div(seg, 4)
    ids = jnp.arange(16, dtype=jnp.int32)
    views = lax.dynamic_slice_in_dim(orders, zl * 4, 4, 0)
    placed = views[:, :, None] == ids[None, None, :]
    placed_len = jnp.sum(jnp.where(placed, lengths[None, None, :], 0), axis=2)
    before = ids[None, :] < ids[:, None]
    starts = RUBRIC_LENGTH + jnp.sum(jnp.where(before[None], placed_len[:, None, :], 0), axis=2)
    offsets = jnp.sum(jnp.where(placed, starts[:, :, None], 0), axis=1)
    wanted = jnp.arange(4, dtype=jnp.int32) * 4 + y
    pick = wanted[:, None] == ids[None, :]
    offsets = jnp.sum(jnp.where(pick[None], offsets[:, None, :], 0), axis=2)
    mine = jnp.sum(jnp.where(pick, lengths[None, :], 0), axis=1)
    mine = jnp.broadcast_to(mine[:, None], (4, 128))
    rows = jnp.arange(ROWS, dtype=jnp.int32)
    query_pos = RUBRIC_LENGTH + jnp.sum(lengths) + rep * ROWS + rows
    rubric_pos = (seg * 2 + rep) * RUB + rows
    cos, sin = tables(jnp.concatenate([query_pos, rubric_pos, offsets.reshape(16)]))
    jcos, jsin = slot_tables()

    V = pltpu.VMEM
    return pl.pallas_call(
        fused_kernel,
        out_shape=jax.ShapeDtypeStruct((ROWS, 1024), BF16),
        in_specs=[ANY] * 11,
        out_specs=VMEM,
        scratch_shapes=[
            V((ROWS, 1024), BF16), V((RUB, 128), BF16), V((SLOTS, 128), BF16),
            V((272, 128), F32), V((272, 128), F32), V((4, 128), jnp.int32),
            V((1024, 128), F32), V((1024, 128), F32),
            V((16, 128, 128), F32), V((16, 128, 128), F32),
            V((4, 1024, 128), BF16), V((8, 2, RUB, 128), BF16), V((8, 2, SLOTS, 128), BF16),
            V((128, 2048), F32), V((128, 2048), BF16), V((2048, 256), BF16), V((128, 128), F32),
            V((4, 1024, 256), F32), V((4, 1024, 128), F32),
            V((4, 1024, 128), BF16), V((4, 8, 128), F32),
            V((4, 1024, 128), BF16), V((4, 8, 128), F32),
            V((4096, 1024), BF16), V((4, 2, ROWS, 1024), BF16),
            V((ROWS, 1024), BF16), V((ROWS, 1024), BF16), V((ROWS, 1024), BF16),
            DMA((10,)), DMA((4,)),
            DMA((4,)), DMA((4,)),
            DMA((2, 4)), DMA((2, 4)),
            DMA((2, 4)), DMA((2, 4)),
            DMA((4,)), DMA((4,)),
            DMA((4,)), DMA((4,)),
            DMA((2,)), DMA((2,)),
            DMA((3, 2)), DMA((3, 2)),
            DMA((3,)), DMA((3,)),
            DMA((3, 2)), DMA((3, 2)),
            DMA((2,)), DMA((2,)),
        ],
        compiler_params=pltpu.CompilerParams(
            collective_id=0, has_side_effects=True, vmem_limit_bytes=58 * 1024 * 1024
        ),
        name="judge",
    )(
        queries, criteria_keys, criteria_values, candidate_keys, candidate_values,
        cos, sin, mine, jnp.asarray(jcos), jnp.asarray(jsin), out_weight,
    )


def solution(mesh):
    rows = P(("seg", "rep"), "head")
    return jax.shard_map(
        local,
        mesh=mesh,
        in_specs=(rows, rows, rows, rows, rows, P(), P(), P("rep", "head")),
        out_specs=rows,
        check_vma=False,
    )
```

time: 166 us -> 111 us (0.67)
  Pallas kernels: 154 us -> 103 us
  local copies, waits for them, and re-layouts: 7.22 us -> 2.4 us
    pallas_call x2 -> x1, Pallas kernels: 154 us -> 103 us  [local(): pl.pallas_call(fused_kernel, out_shape=jax.ShapeDtypeStruct((ROWS, 1024),...]
    unnamed x17 -> x3, local copies, waits for them, and re-layouts: 7.06 us -> 1.67 us
where the time goes in v2:
time: 111 us
  Pallas kernels  103 us (93%)
  other arithmetic  4.89 us (4%)
  local copies, waits for them, and re-layouts  2.4 us (2%)
    pallas_call x1, Pallas kernels, local(): pl.pallas_call(fused_kernel, out_shape=jax.ShapeDtypeStruct((ROWS, 1024),...  103 us

profile of v2, /device:TPU:42, one launch (start us, length us, event | category | flops | bytes accessed | tf_op | source)
XLA Modules:
  0.0 111.2 jit_solution(11524537023321868102)
XLA Ops:
  0.0 0.0 copy-start
  0.0 1.3 %reduce_sum.54 = s32[]{:T(128)} reduce(s32[16]{0:T(128)} %param.15, s32[]{:T(128)} %constant.16.clone.1), dimensions={0}, to_apply=%region_0.1 | reduce | flops 15 | bytes 72 | tf_op jit(solution)/shard_map/reduce_sum | solution.py:472
  2.0 0.8 select_reduce_fusion.4
  2.8 0.1 iota_compare_fusion.2
  2.9 0.1 compare_select_fusion
  3.0 0.0 copy-done
  3.0 0.6 broadcast_in_dim.114.len_ref
  3.6 0.9 select_reduce_fusion.2
  4.5 0.1 select_reduce_fusion.1
  4.7 0.1 select_reduce_fusion
  4.8 0.2 select_reduce_fusion.3
  4.9 0.1 concatenate.12
  5.0 1.3 %fusion = (f32[272,128]{1,0:T(8,128)}, f32[272,128]{1,0:T(8,128)}) fusion(f32[128]{0:T(128)S(1)} %get-tuple-element.9, f32[128]{0:T(128)S(1)} %get-tuple-element.10, f32[272]{0:T(512)S(1)} %add_convert_fusion), kind=kLoop, calls=%fused_computation.2 | loop fusion | flops 69632 | bytes 280640 | tf_op jit(solution)/shard_map/mul | solution.py:37
  6.3 103.2 %judge.1 = bf16[128,1024]{1,0:T(8,128)(2,1)} custom-call(bf16[128,1024]{1,0:T(8,128)(2,1)} %q_ref.1, bf16[128,128]{1,0:T(8,128)(2,1)} %rk_ref.1, bf16[128,128]{1,0:T(8,128)(2,1)} %rv_ref.1, bf16[512,128]{1,0:T(8,128)(2,1)} %ck_ref.1, bf16[512,128]{1,0:T(8,128)(2,1)} %cv_ref.1, f32[272,128]{1,0:T(8,128)} %get-tuple-element.6.cos_ref, ...), custom_call_target="tpu_custom_call" | custom-call | tf_op jit(solution)/shard_map/judge/pallas_call | solution.py:478
  109.5 1.7 %copy.12 = bf16[128,1024]{1,0:T(8,128)(2,1)} copy(bf16[128,1024]{1,0:T(8,128)(2,1)} %judge.1) | data formatting | bytes 524288
  (7 shorter events, 0.1 us)
Async XLA Ops:
  0.0 3.0 %copy-start = (s32[16,16]{1,0:T(8,128)S(1)}, s32[16,16]{1,0:T(8,128)}, u32[]{:S(2)}) copy-start(s32[16,16]{1,0:T(8,128)} %param.16) | copy-start | bytes 3076

commit v3 on v2

v3 whole, which is shorter than its diff:
```python
import functools
import math

import jax
import jax.numpy as jnp
import numpy as np
from jax import lax
from jax.experimental import pallas as pl
from jax.experimental.pallas import tpu as pltpu
from jax.sharding import PartitionSpec as P

QUERY_HEADS = 64
KEY_VALUE_HEADS = 8
HEAD_WIDTH = 128
ANSWER_LENGTH = 1024
RUBRIC_LENGTH = 4096
THETA = 1000000.0
GROUP = 8
ROWS = 128
SLOTS = 512
RUB = 128
CHUNK = 64
LIVE_TOTAL = 10240
QUERY_START = RUBRIC_LENGTH + LIVE_TOTAL
SHARD = SLOTS + RUB
HALF = GROUP * CHUNK
SCALE = math.log2(math.e) / math.sqrt(HEAD_WIDTH)
MESH = pl.DeviceIdType.MESH
F32 = jnp.float32
BF16 = jnp.bfloat16


def tables(pos):
    halfway = HEAD_WIDTH // 2
    frequency = jnp.exp(
        jnp.arange(halfway, dtype=F32) * (-2.0 * math.log(THETA) / HEAD_WIDTH)
    )
    frequency = jnp.concatenate([frequency, frequency])
    angles = pos.astype(F32)[:, None] * frequency[None, :]
    sign = jnp.where(jnp.arange(HEAD_WIDTH) < halfway, -1.0, 1.0).astype(F32)
    return jnp.cos(angles), jnp.sin(angles) * sign[None, :]


def angle_tables():
    halfway = HEAD_WIDTH // 2
    exponent = np.arange(halfway, dtype=np.float32) * np.float32(-2.0 * math.log(THETA) / HEAD_WIDTH)
    frequency = np.exp(exponent).astype(np.float32)
    positions = np.concatenate([
        np.arange(RUBRIC_LENGTH), QUERY_START + np.arange(2 * ROWS),     ]).astype(np.float32)
    angles = (positions[:, None] * frequency[None, :]).astype(np.float64)
    cos, sin = np.cos(angles), np.sin(angles)
    return (
        np.concatenate([cos, cos], axis=1).astype(np.float32),
        np.concatenate([-sin, sin], axis=1).astype(np.float32),
    )


def turn(x, cos, sin):
    return x * cos + pltpu.roll(x, HEAD_WIDTH // 2, 1) * sin


def fused_kernel(
    q_ref, rk_ref, rv_ref, ck_ref, cv_ref, cos_ref, sin_ref, w_ref, len_ref, hcos_ref, hsin_ref,
    out_ref,
    lens, qin, cvin, rvin, ckin, rkin, jcos, jsin, hcos, hsin, qcos, qsin, rcos, rsin, ocos, osin,
    qbuf, kbuf, vbuf, kjt, kkt, vaug, live_col, acc, peak, obuf, lbuf, osend, lsend,
    wbuf, fbuf, att, part, got,
    ins, ws, qs, qr, cs, cr, os, orr, ls, lr,
    zsend, zrecv, xs, xr, fs, fr, ds, dr, ps, pr,
):
    seg = lax.axis_index("seg")
    rep = lax.axis_index("rep")
    head = lax.axis_index("head")
    y = lax.rem(seg, 4)
    zl = lax.div(seg, 4)
    z = rep * 4 + zl
    x = lax.div(head, 2)
    core = lax.rem(head, 2)

    def at(yy, zz):
        yy = lax.rem(yy + 8, 4)
        zz = lax.rem(zz + 16, 8)
        return {"seg": lax.rem(zz, 4) * 4 + yy, "rep": lax.div(zz, 4)}

    def zs(d):
        return lax.rem(z + d + 16, 8)

    def ys(d):
        return lax.rem(y + d + 8, 4)

    def copy(src, dst, ssem, rsem, dev):
        return pltpu.make_async_remote_copy(
            src_ref=src, dst_ref=dst, send_sem=ssem, recv_sem=rsem,
            device_id=dev, device_id_type=MESH,
        )

    def start(pair):
        for c in pair:
            c.start()

    def arrived(pair):
        for c in pair:
            c.wait_recv()

    mine_rows = pl.ds((seg * 2 + rep) * RUB, RUB)
    query_rows = pl.ds(RUBRIC_LENGTH + rep * ROWS, ROWS)
    low_rows = pl.ds(0, 1024)
    load = [
        pltpu.make_async_copy(a, b, ins.at[i])
        for i, (a, b) in enumerate((
            (cv_ref, cvin), (rv_ref, rvin),
            (q_ref, qin), (cos_ref.at[query_rows], qcos), (sin_ref.at[query_rows], qsin),
            (ck_ref, ckin), (rk_ref, rkin),
            (cos_ref.at[mine_rows], rcos), (sin_ref.at[mine_rows], rsin),
            (hcos_ref, hcos), (hsin_ref, hsin), (len_ref, lens),
            (cos_ref.at[low_rows], jcos), (sin_ref.at[low_rows], jsin),
        ))
    ]
    start(load)

    up, down = at(y, z + 1), at(y, z - 1)
    north, south, beyond = at(y + 1, z), at(y - 1, z), at(y + 2, z)
    east = {"head": lax.rem(x + 1, 4) * 2 + core}
    west = {"head": lax.rem(x + 3, 4) * 2 + core}
    other = {"head": x * 2 + 1 - core}
    partner = {"rep": 1 - rep}
    barrier = pltpu.get_barrier_semaphore()
    peers = (up, down, north, south, beyond, east, west, other, partner)
    for dev in peers:
        pl.semaphore_signal(barrier, inc=1, device_id=dev, device_id_type=MESH)
    pl.semaphore_wait(barrier, len(peers))

    def ring(step, c):
        a, b = zs(-step), zs(step)
        buf = (kbuf, vbuf)[c]
        ahead = copy(buf.at[a], buf.at[a], cs.at[0, step * 2 + c], cr.at[0, step * 2 + c], up)
        back = copy(buf.at[b], buf.at[b], cs.at[1, step * 2 + c], cr.at[1, step * 2 + c], down)
        if step < 3:
            return (ahead, back)
        return (ahead,) if c == 1 else (back,)

    rings = [[ring(s, c) for c in range(2)] for s in range(4)]

    def forward(step, c):
        arrived(rings[step][c])
        start(rings[step + 1][c])

    for c in load[:2]:
        c.wait()
    vbuf[z, 0:SLOTS, :] = cvin[...]
    vbuf[z, SLOTS:SHARD, :] = rvin[...]
    start(rings[0][1])
    for c in load[2:5]:
        c.wait()
    cq, sq = qcos[...], qsin[...]
    for h in range(GROUP):
        v = turn(qin[:, h * 128 : (h + 1) * 128].astype(F32), cq, sq).astype(BF16)
        qbuf[y, h * CHUNK : (h + 1) * CHUNK, :] = v[:CHUNK]
        qbuf[y, HALF + h * CHUNK : HALF + (h + 1) * CHUNK, :] = v[CHUNK:]
    qdir = (
        copy(qbuf.at[y], qbuf.at[y], qs.at[0], qr.at[0], north),
        copy(qbuf.at[y], qbuf.at[y], qs.at[1], qr.at[1], south),
    )
    start(qdir)
    for c in load[5:9]:
        c.wait()
    kbuf[z, 0:SLOTS, :] = ckin[...]
    kbuf[z, SLOTS:SHARD, :] = turn(rkin[...].astype(F32), rcos[...], rsin[...]).astype(BF16)
    start(rings[0][0])
    south_slot, north_slot = ys(-1), ys(1)
    qfwd = (
        copy(qbuf.at[south_slot, 0:HALF], qbuf.at[south_slot, 0:HALF], qs.at[2], qr.at[2], north),
        copy(qbuf.at[north_slot, HALF:], qbuf.at[north_slot, HALF:], qs.at[3], qr.at[3], south),
    )
    wload = [
        pltpu.make_async_copy(w_ref.at[pl.ds(i * 1024, 1024)], wbuf.at[pl.ds(i * 1024, 1024)], ws.at[i])
        for i in range(4)
    ]
    start(wload)
    for c in load[9:]:
        c.wait()

    for i in range(16):
        ocos[i] = jnp.broadcast_to(hcos[i : i + 1, :], (128, 128)).T
        osin[i] = jnp.broadcast_to(hsin[i : i + 1, :], (128, 128)).T
    live_col[...] = jnp.broadcast_to(kbuf[z, SLOTS : SLOTS + 16, :][0:1].astype(F32), (128, 128)).T

    lane = lax.broadcasted_iota(jnp.int32, (128, 128), 1)
    row = lax.broadcasted_iota(jnp.int32, (SLOTS, HEAD_WIDTH), 0)

    def prepare(shards, kkt, count=3, first=0):
        for n, zz in enumerate(shards, first):
            slots = slice(n * SLOTS, (n + 1) * SLOTS)
            rubric = slice(count * SLOTS + n * RUB, count * SLOTS + (n + 1) * RUB)
            place = lax.div(zz, 4) * SLOTS
            rows = pl.ds(pl.multiple_of(place, SLOTS), SLOTS)
            length = lens[pl.ds(lax.rem(zz, 4), 1), :]
            kjt[:, slots] = turn(kbuf[zz, 0:SLOTS, :].astype(F32), jcos[rows, :], jsin[rows, :]).T
            kkt[:, rubric] = kbuf[zz, SLOTS:SHARD, :].astype(F32).T.astype(BF16)
            alive = row + place < length
            vaug[slots, 0:128] = jnp.where(alive, vbuf[zz, 0:SLOTS, :].astype(F32), 0.0).astype(BF16)
            vaug[slots, 128:256] = jnp.where(alive, 1.0, 0.0).astype(BF16)
            vaug[rubric, 0:128] = vbuf[zz, SLOTS:SHARD, :]
            vaug[rubric, 128:256] = jnp.ones((RUB, 128), BF16)

    def rotate(shards, slot, kkt):
        for n, zz in enumerate(shards):
            length = lens[pl.ds(lax.rem(zz, 4), 1), :]
            place = lax.div(zz, 4) * SLOTS
            co, so = ocos[slot * 4 + lax.rem(zz, 4)], osin[slot * 4 + lax.rem(zz, 4)]
            for i in range(SLOTS // 128):
                cols = slice(n * SLOTS + i * 128, n * SLOTS + (i + 1) * 128)
                k = kjt[:, cols]
                k = k * co + jnp.concatenate([k[64:], k[:64]], axis=0) * so
                alive = lane + (place + i * 128) < length
                kkt[:, cols] = jnp.where(alive, k, live_col[...]).astype(BF16)

    def share_rubric(n):
        kkt[n, :, 3 * SLOTS : 3 * SHARD] = kkt[0, :, 3 * SLOTS : 3 * SHARD]

    def flash(slot, keys, kkt, first=False, tiles=range(4)):
        scores = [
            jnp.dot(qbuf[slot, i * 256 : (i + 1) * 256, :], kkt[:, 0:keys], preferred_element_type=F32)
            for i in tiles
        ]
        for s, i in zip(scores, tiles):
            rows = slice(i * 256, (i + 1) * 256)
            top = jnp.max(s, axis=1, keepdims=True) * SCALE
            if first:
                new = jnp.broadcast_to(top, (256, 128))
            else:
                old = peak[slot, rows, :]
                new = jnp.maximum(old, top)
            p = jnp.exp2(s * SCALE - new[:, 0:1]).astype(BF16)
            o = jnp.dot(p, vaug[0:keys, :], preferred_element_type=F32)
            if first:
                acc[slot, rows, :] = o
            else:
                f = jnp.exp2(old - new)
                acc[slot, rows, 0:128] = acc[slot, rows, 0:128] * f + o[:, 0:128]
                acc[slot, rows, 128:256] = acc[slot, rows, 128:256] * f + o[:, 128:256]
            peak[slot, rows, :] = new

    near = (z, zs(-1), zs(1))

    def ordered(n, base):
        return lax.rem(y + base + 3 * n + 3 * lax.div(n, 2) + 2 * lax.div(n, 3), 4)

    one = kkt.at[0]
    prepare(near[:1], one)
    forward(0, 1)
    arrived(qdir)
    start(qfwd)
    forward(0, 0)
    prepare(near[1:], one, 3, 1)

    def unit_near(n, carry):
        slot = ordered(n, 0)

        @pl.when(n == 2)
        def _():
            forward(1, 1)

        @pl.when(n == 3)
        def _():
            forward(1, 0)
            arrived(qfwd)

        rotate(near, slot, one)
        flash(slot, 3 * SHARD, one, True)
        return carry

    lax.fori_loop(0, 4, unit_near, 0)

    forward(2, 1)
    second = (zs(-2), zs(2))
    prepare(second, one, 2)

    def unit_second(n, carry):
        slot = lax.rem(y + n, 4)

        @pl.when(n == 2)
        def _():
            forward(2, 0)

        rotate(second, slot, one)
        flash(slot, 2 * SHARD, one)
        return carry

    lax.fori_loop(0, 4, unit_second, 0)

    eye = lax.broadcasted_iota(jnp.int32, (CHUNK, 128), 0) == lax.broadcasted_iota(jnp.int32, (CHUNK, 128), 1)

    def outgoing(i, n, dev):
        return (
            copy(osend.at[i, n], obuf.at[i, n], os.at[i, n], orr.at[i, n], dev),
            copy(lsend.at[i, n], lbuf.at[i, n], ls.at[i, n], lr.at[i, n], dev),
        )

    def finish(i, n, slot):
        for h in range(GROUP):
            rows = slice(i * HALF + h * CHUNK, i * HALF + (h + 1) * CHUNK)
            total = acc[slot, rows, 128:256]
            stat = peak[slot, rows, :] + jnp.log2(total)
            osend[i, n, h * CHUNK : (h + 1) * CHUNK, :] = (acc[slot, rows, 0:128] / total).astype(BF16)
            lsend[i, n, h : h + 1, :] = jnp.sum(jnp.where(eye, stat, 0.0), axis=0, keepdims=True)

        @pl.when(n != 3)
        def _():
            start(outgoing(i, n, at(slot, z)))

    def last_slot(n):
        return ordered(n, 2)

    partials = [
        [outgoing(i, 0, beyond), outgoing(i, 1, north), outgoing(i, 2, south)] for i in range(2)
    ]

    def combine(i):
        for pair in partials[i]:
            arrived(pair)
        stats = [lbuf[i, 0], lbuf[i, 1], lbuf[i, 2], lsend[i, 3]]
        top = functools.reduce(jnp.maximum, stats)
        parts = [jnp.exp2(s - top) for s in stats]
        total = parts[0] + parts[1] + parts[2] + parts[3]
        shares = [jnp.concatenate([p / total] * 16, axis=0).T for p in parts]
        for h in range(GROUP):
            rows = slice(h * CHUNK, (h + 1) * CHUNK)
            out = None
            for n in range(4):
                src = osend[i, 3, rows, :] if n == 3 else obuf[i, n, rows, :]
                term = shares[n][0:CHUNK, h : h + 1] * src.astype(F32)
                out = term if out is None else out + term
            att[i, :, h * 128 : (h + 1) * 128] = out.astype(BF16)

    half = lax.div(head, 4)
    mine = half == rep
    u = lax.rem(x - 2 * rep + 8, 4)
    g = lax.rem(head, 4)
    far = 1 - rep

    swaps = [
        copy(att.at[i], fbuf.at[g, rep, i], zsend.at[i], zrecv.at[i], partner)
        for i in range(2)
    ]
    swapped = [
        copy(fbuf.at[g, far, i], fbuf.at[g, far, i], zsend.at[i], zrecv.at[i], partner)
        for i in range(2)
    ]

    def block(k, n):
        return fbuf.at[k, rep if n < 2 else far, n % 2]

    def hop(blk, n, way):
        return copy(blk, blk, xs.at[n, way], xr.at[n, way], (east, west)[way])

    def cross(blk, n, way):
        return copy(blk, blk, ds.at[n, way], dr.at[n, way], other)

    def spread(n):
        blk = block(g, n)
        start((hop(blk, n, 0), hop(blk, n, 1), cross(blk, n, 0)))

    def publish(i):
        combine(i)

        @pl.when(mine)
        def _():
            fbuf[g, rep, i] = att[i]
            spread(i)

        @pl.when(jnp.logical_not(mine))
        def _():
            swaps[i].start()

    low, high = core, 2 + core
    roles = ((low, high), (high, low), (high, low), (low, high))

    def collect(n):
        for which, (k0, k1) in enumerate(roles):

            @pl.when(u == which)
            def _():
                if which < 2:
                    blk = block(k1, n)
                    hop(blk, n, 1 - which).wait_recv()
                    cross(blk, n, 1).start()
                else:
                    way = which - 2
                    blk, blk1 = block(k0, n), block(k1, n)
                    hop(blk, n, way).wait_recv()
                    start((copy(blk, blk, fs.at[n], fr.at[n], (east, west)[way]), cross(blk, n, 0)))
                    copy(blk1, blk1, fs.at[n], fr.at[n], (east, west)[way]).wait_recv()
                    cross(blk1, n, 1).start()

    def crossed(n):
        blk = block(g, n)
        cross(blk, n, 0).wait_recv()
        cross(blk, n, 1).wait_recv()

    def product(r, i):
        total = None
        for k in range(4):
            term = jnp.dot(
                fbuf[k, r, i], wbuf[k * 1024 : (k + 1) * 1024, :], preferred_element_type=F32
            )
            total = term if total is None else total + term
        return total

    arrived(rings[3][0])
    arrived(rings[3][1])
    last = (zs(-3), zs(3), zs(4))
    for n in range(4):
        prepare(last, kkt.at[n], 3) if n == 0 else share_rubric(n)

    def unit_last(n, carry):
        slot = last_slot(n)
        rotate(last, slot, kkt.at[n])
        flash(slot, 3 * SHARD, kkt.at[n], tiles=(0, 1))
        finish(0, n, slot)
        return carry

    lax.fori_loop(0, 4, unit_last, 0)

    def unit_end(n, carry):
        slot = last_slot(n)

        @pl.when(n == 2)
        def _():
            publish(0)

        flash(slot, 3 * SHARD, kkt.at[n], tiles=(2, 3))
        finish(1, n, slot)
        return carry

    lax.fori_loop(0, 4, unit_end, 0)
    collect(0)
    publish(1)
    collect(1)
    for c in wload:
        c.wait()
    sends = []
    for i in range(2):

        @pl.when(mine)
        def _():
            swapped[i].wait_recv()
            spread(2 + i)

        collect(2 + i)
        crossed(2 + i)
        part[i] = product(far, i).astype(BF16)
        c = copy(part.at[i], got.at[i], ps.at[i], pr.at[i], partner)
        c.start()
        sends.append(c)
    crossed(0)
    crossed(1)
    own = [product(rep, i) for i in range(2)]
    for i in range(2):
        rows = slice(i * CHUNK, (i + 1) * CHUNK)
        sends[i].wait_recv()
        out_ref[rows, :] = (own[i] + got[i].astype(F32)).astype(BF16)

    for pairs in (*rings, (qdir, qfwd), *partials, (sends,)):
        for pair in pairs:
            for c in pair:
                c.wait_send()
    for n in range(4):
        blk = block(g, n)
        cross(blk, n, 0).wait_send()
        cross(blk, n, 1).wait_send()

    @pl.when(mine)
    def _():
        for n in range(4):
            hop(block(g, n), n, 0).wait_send()
            hop(block(g, n), n, 1).wait_send()

    @pl.when(jnp.logical_not(mine))
    def _():
        for n in range(4):
            blk = block(g, n)
            copy(blk, blk, fs.at[n], fr.at[n], east).wait_send()
        for c in swaps:
            c.wait_send()


VMEM = pl.BlockSpec(memory_space=pltpu.VMEM)
ANY = pl.BlockSpec(memory_space=pl.ANY)
DMA = pltpu.SemaphoreType.DMA


def local(
    queries, criteria_keys, criteria_values, candidate_keys, candidate_values,
    lengths, orders, out_weight,
):
    seg = lax.axis_index("seg")
    y, zl = lax.rem(seg, 4), lax.div(seg, 4)
    ids = jnp.arange(16, dtype=jnp.int32)
    views = lax.dynamic_slice_in_dim(orders, zl * 4, 4, 0)
    placed = views[:, :, None] == ids[None, None, :]
    placed_len = jnp.sum(jnp.where(placed, lengths[None, None, :], 0), axis=2)
    before = ids[None, :] < ids[:, None]
    starts = RUBRIC_LENGTH + jnp.sum(jnp.where(before[None], placed_len[:, None, :], 0), axis=2)
    offsets = jnp.sum(jnp.where(placed, starts[:, :, None], 0), axis=1)
    wanted = jnp.arange(4, dtype=jnp.int32) * 4 + y
    pick = wanted[:, None] == ids[None, :]
    offsets = jnp.sum(jnp.where(pick[None], offsets[:, None, :], 0), axis=2)
    mine = jnp.sum(jnp.where(pick, lengths[None, :], 0), axis=1)
    mine = jnp.broadcast_to(mine[:, None], (4, 128))
    hcos, hsin = tables(offsets.reshape(16))
    cos, sin = angle_tables()
    V = pltpu.VMEM
    return pl.pallas_call(
        fused_kernel,
        out_shape=jax.ShapeDtypeStruct((ROWS, 1024), BF16),
        in_specs=[ANY] * 11,
        out_specs=VMEM,
        scratch_shapes=[
            V((4, 128), jnp.int32), V((ROWS, 1024), BF16), V((SLOTS, 128), BF16), V((RUB, 128), BF16), V((SLOTS, 128), BF16),
            V((RUB, 128), BF16), V((1024, 128), F32), V((1024, 128), F32),
            V((16, 128), F32), V((16, 128), F32), V((128, 128), F32), V((128, 128), F32), V((128, 128), F32), V((128, 128), F32),
            V((16, 128, 128), F32), V((16, 128, 128), F32),
            V((4, 1024, 128), BF16), V((8, SHARD, 128), BF16), V((8, SHARD, 128), BF16),
            V((128, 3 * SLOTS), F32), V((4, 128, 3 * SHARD), BF16), V((3 * SHARD, 256), BF16), V((128, 128), F32),
            V((4, 1024, 256), F32), V((4, 1024, 128), F32),
            V((2, 4, HALF, 128), BF16), V((2, 4, 8, 128), F32),
            V((2, 4, HALF, 128), BF16), V((2, 4, 8, 128), F32),
            V((4096, 1024), BF16), V((4, 2, 2, CHUNK, 1024), BF16),
            V((2, CHUNK, 1024), BF16), V((2, CHUNK, 1024), BF16), V((2, CHUNK, 1024), BF16),
            DMA((14,)), DMA((4,)),
            DMA((4,)), DMA((4,)),
            DMA((2, 8)), DMA((2, 8)),
            DMA((2, 4)), DMA((2, 4)),
            DMA((2, 4)), DMA((2, 4)),
            DMA((2,)), DMA((2,)),
            DMA((4, 2)), DMA((4, 2)),
            DMA((4,)), DMA((4,)),
            DMA((4, 2)), DMA((4, 2)),
            DMA((2,)), DMA((2,)),
        ],
        compiler_params=pltpu.CompilerParams(
            collective_id=0, has_side_effects=True, vmem_limit_bytes=58 * 1024 * 1024
        ),
        name="judge",
    )(
        queries, criteria_keys, criteria_values, candidate_keys, candidate_values,
        jnp.asarray(cos), jnp.asarray(sin), out_weight, mine, hcos, hsin,
    )


def solution(mesh):
    rows = P(("seg", "rep"), "head")
    return jax.shard_map(
        local,
        mesh=mesh,
        in_specs=(rows, rows, rows, rows, rows, P(), P(), P("rep", "head")),
        out_specs=rows,
        check_vma=False,
    )
```

time: 111 us -> 97.7 us (0.88)
  the two profiles are of different devices: /device:TPU:42 before, /device:TPU:33 now
where the time goes in v3:
time: 97.7 us; the launch traced here: 97.5 us
  Pallas kernels  92.1 us (94%)
  other arithmetic  3.02 us (3%)
  local copies, waits for them, and re-layouts  2.42 us (2%)
    pallas_call x1, Pallas kernels, local(): pl.pallas_call(fused_kernel, out_shape=jax.ShapeDtypeStruct((ROWS, 1024),...  92.1 us

profile of v3, /device:TPU:33, one launch (start us, length us, event | category | flops | bytes accessed | tf_op | source)
XLA Modules:
  0.0 97.5 jit_solution(9631361210072554382)
XLA Ops:
  0.0 0.0 copy-start
  0.0 0.8 select_reduce_fusion.4
  0.9 0.1 iota_compare_fusion.2
  0.9 0.1 compare_select_fusion
  1.0 0.0 copy-done
  1.0 0.7 broadcast_in_dim.104.len_ref
  1.7 0.9 select_reduce_fusion.2
  2.6 0.1 select_reduce_fusion.1
  2.7 0.1 select_reduce_fusion
  2.8 0.2 select_reduce_fusion.3
  3.0 0.1 convert_element_type.11
  3.1 0.7 fusion
  3.8 92.1 %judge.1 = bf16[128,1024]{1,0:T(8,128)(2,1)} custom-call(bf16[128,1024]{1,0:T(8,128)(2,1)} %q_ref.1, bf16[128,128]{1,0:T(8,128)(2,1)} %rk_ref.1, bf16[128,128]{1,0:T(8,128)(2,1)} %rv_ref.1, bf16[512,128]{1,0:T(8,128)(2,1)} %ck_ref.1, bf16[512,128]{1,0:T(8,128)(2,1)} %cv_ref.1, f32[4352,128]{1,0:T(8,128)} %constant.32.clone.cos_ref, ...), custom_call_target="tpu_custom_call" | custom-call | tf_op jit(solution)/shard_map/judge/pallas_call | solution.py:514
  95.9 1.7 %copy.12 = bf16[128,1024]{1,0:T(8,128)(2,1)} copy(bf16[128,1024]{1,0:T(8,128)(2,1)} %judge.1) | data formatting | bytes 524288
  (6 shorter events, 0.0 us)
Async XLA Ops:
  0.0 1.0 %copy-start = (s32[16,16]{1,0:T(8,128)S(1)}, s32[16,16]{1,0:T(8,128)}, u32[]{:S(2)}) copy-start(s32[16,16]{1,0:T(8,128)} %param.16) | copy-start | bytes 3076

commit v4 on v3

--- a/solution.py
+++ b/solution.py
@@ -30,23 +30,13 @@
 BF16 = jnp.bfloat16
 
 
-def tables(pos):
-    halfway = HEAD_WIDTH // 2
-    frequency = jnp.exp(
-        jnp.arange(halfway, dtype=F32) * (-2.0 * math.log(THETA) / HEAD_WIDTH)
-    )
-    frequency = jnp.concatenate([frequency, frequency])
-    angles = pos.astype(F32)[:, None] * frequency[None, :]
-    sign = jnp.where(jnp.arange(HEAD_WIDTH) < halfway, -1.0, 1.0).astype(F32)
-    return jnp.cos(angles), jnp.sin(angles) * sign[None, :]
-
-
 def angle_tables():
     halfway = HEAD_WIDTH // 2
     exponent = np.arange(halfway, dtype=np.float32) * np.float32(-2.0 * math.log(THETA) / HEAD_WIDTH)
     frequency = np.exp(exponent).astype(np.float32)
     positions = np.concatenate([
-        np.arange(RUBRIC_LENGTH), QUERY_START + np.arange(2 * ROWS),     ]).astype(np.float32)
+        np.arange(RUBRIC_LENGTH), QUERY_START + np.arange(2 * ROWS), 128 * np.arange(128),
+    ]).astype(np.float32)
     angles = (positions[:, None] * frequency[None, :]).astype(np.float64)
     cos, sin = np.cos(angles), np.sin(angles)
     return (
@@ -60,9 +50,9 @@
 
 
 def fused_kernel(
-    q_ref, rk_ref, rv_ref, ck_ref, cv_ref, cos_ref, sin_ref, w_ref, len_ref, hcos_ref, hsin_ref,
+    q_ref, rk_ref, rv_ref, ck_ref, cv_ref, cos_ref, sin_ref, w_ref, len_ref, order_ref,
     out_ref,
-    lens, qin, cvin, rvin, ckin, rkin, jcos, jsin, hcos, hsin, qcos, qsin, rcos, rsin, ocos, osin,
+    len_in, order_in, lens, offs, qin, cvin, rvin, ckin, rkin, jcos, jsin, hcos, hsin, qcos, qsin, rcos, rsin, ocos, osin,
     qbuf, kbuf, vbuf, kjt, kkt, vaug, live_col, acc, peak, obuf, lbuf, osend, lsend,
     wbuf, fbuf, att, part, got,
     ins, ws, qs, qr, cs, cr, os, orr, ls, lr,
@@ -104,6 +94,7 @@
 
     mine_rows = pl.ds((seg * 2 + rep) * RUB, RUB)
     query_rows = pl.ds(RUBRIC_LENGTH + rep * ROWS, ROWS)
+    high_rows = pl.ds(RUBRIC_LENGTH + 2 * ROWS, 128)
     low_rows = pl.ds(0, 1024)
     load = [
         pltpu.make_async_copy(a, b, ins.at[i])
@@ -112,7 +103,8 @@
             (q_ref, qin), (cos_ref.at[query_rows], qcos), (sin_ref.at[query_rows], qsin),
             (ck_ref, ckin), (rk_ref, rkin),
             (cos_ref.at[mine_rows], rcos), (sin_ref.at[mine_rows], rsin),
-            (hcos_ref, hcos), (hsin_ref, hsin), (len_ref, lens),
+            (cos_ref.at[high_rows], hcos), (sin_ref.at[high_rows], hsin),
+            (len_ref, len_in), (order_ref, order_in),
             (cos_ref.at[low_rows], jcos), (sin_ref.at[low_rows], jsin),
         ))
     ]
@@ -180,9 +172,33 @@
     for c in load[9:]:
         c.wait()
 
+    place_row = lax.broadcasted_iota(jnp.int32, (128, 128), 0)
+
+    def row_of(table, index):
+        return jnp.sum(jnp.where(place_row == index, table[0:128, :], 0.0), axis=0, keepdims=True)
+
+    first = lax.broadcasted_iota(jnp.int32, (16, 16), 0)
+    second_index = lax.broadcasted_iota(jnp.int32, (16, 16), 1)
+    same = first == second_index
+
+    def column(values):
+        return jnp.sum(jnp.where(same, values, 0.0), axis=1, keepdims=True)
+
+    len_col = column(len_in[...].astype(F32))
+    lens[...] = jnp.broadcast_to(len_col, (16, 128)).astype(jnp.int32)
+    for a in range(4):
+        placed = first == order_in[pl.ds(zl * 4 + a, 1), :]
+        placed_len = jnp.sum(jnp.where(placed, len_col, 0.0), axis=0, keepdims=True)
+        before = jnp.sum(jnp.where(first < second_index, column(placed_len), 0.0), axis=0, keepdims=True)
+        offset = RUBRIC_LENGTH + jnp.sum(jnp.where(placed, before, 0.0), axis=1, keepdims=True)
+        offs[a] = jnp.broadcast_to(offset, (16, 128)).astype(jnp.int32)
     for i in range(16):
-        ocos[i] = jnp.broadcast_to(hcos[i : i + 1, :], (128, 128)).T
-        osin[i] = jnp.broadcast_to(hsin[i : i + 1, :], (128, 128)).T
+        offset = offs[i // 4, pl.ds(i % 4 * 4 + y, 1), :]
+        hi, lo = lax.shift_right_logical(offset, 7), lax.bitwise_and(offset, 127)
+        ch, sh = row_of(hcos, hi), row_of(hsin, hi)
+        cl, sl = row_of(jcos, lo), row_of(jsin, lo)
+        ocos[i] = jnp.broadcast_to(ch * cl - sh * sl, (128, 128)).T
+        osin[i] = jnp.broadcast_to(sh * cl + ch * sl, (128, 128)).T
     live_col[...] = jnp.broadcast_to(kbuf[z, SLOTS : SLOTS + 16, :][0:1].astype(F32), (128, 128)).T
 
     lane = lax.broadcasted_iota(jnp.int32, (128, 128), 1)
@@ -194,7 +210,7 @@
             rubric = slice(count * SLOTS + n * RUB, count * SLOTS + (n + 1) * RUB)
             place = lax.div(zz, 4) * SLOTS
             rows = pl.ds(pl.multiple_of(place, SLOTS), SLOTS)
-            length = lens[pl.ds(lax.rem(zz, 4), 1), :]
+            length = lens[pl.ds(lax.rem(zz, 4) * 4 + y, 1), :]
             kjt[:, slots] = turn(kbuf[zz, 0:SLOTS, :].astype(F32), jcos[rows, :], jsin[rows, :]).T
             kkt[:, rubric] = kbuf[zz, SLOTS:SHARD, :].astype(F32).T.astype(BF16)
             alive = row + place < length
@@ -205,7 +221,7 @@
 
     def rotate(shards, slot, kkt):
         for n, zz in enumerate(shards):
-            length = lens[pl.ds(lax.rem(zz, 4), 1), :]
+            length = lens[pl.ds(lax.rem(zz, 4) * 4 + y, 1), :]
             place = lax.div(zz, 4) * SLOTS
             co, so = ocos[slot * 4 + lax.rem(zz, 4)], osin[slot * 4 + lax.rem(zz, 4)]
             for i in range(SLOTS // 128):
@@ -494,32 +510,18 @@
     queries, criteria_keys, criteria_values, candidate_keys, candidate_values,
     lengths, orders, out_weight,
 ):
-    seg = lax.axis_index("seg")
-    y, zl = lax.rem(seg, 4), lax.div(seg, 4)
-    ids = jnp.arange(16, dtype=jnp.int32)
-    views = lax.dynamic_slice_in_dim(orders, zl * 4, 4, 0)
-    placed = views[:, :, None] == ids[None, None, :]
-    placed_len = jnp.sum(jnp.where(placed, lengths[None, None, :], 0), axis=2)
-    before = ids[None, :] < ids[:, None]
-    starts = RUBRIC_LENGTH + jnp.sum(jnp.where(before[None], placed_len[:, None, :], 0), axis=2)
-    offsets = jnp.sum(jnp.where(placed, starts[:, :, None], 0), axis=1)
-    wanted = jnp.arange(4, dtype=jnp.int32) * 4 + y
-    pick = wanted[:, None] == ids[None, :]
-    offsets = jnp.sum(jnp.where(pick[None], offsets[:, None, :], 0), axis=2)
-    mine = jnp.sum(jnp.where(pick, lengths[None, :], 0), axis=1)
-    mine = jnp.broadcast_to(mine[:, None], (4, 128))
-    hcos, hsin = tables(offsets.reshape(16))
     cos, sin = angle_tables()
     V = pltpu.VMEM
     return pl.pallas_call(
         fused_kernel,
         out_shape=jax.ShapeDtypeStruct((ROWS, 1024), BF16),
-        in_specs=[ANY] * 11,
+        in_specs=[ANY] * 10,
         out_specs=VMEM,
         scratch_shapes=[
-            V((4, 128), jnp.int32), V((ROWS, 1024), BF16), V((SLOTS, 128), BF16), V((RUB, 128), BF16), V((SLOTS, 128), BF16),
+            V((1, 16), jnp.int32), V((16, 16), jnp.int32), V((16, 128), jnp.int32), V((4, 16, 128), jnp.int32),
+            V((ROWS, 1024), BF16), V((SLOTS, 128), BF16), V((RUB, 128), BF16), V((SLOTS, 128), BF16),
             V((RUB, 128), BF16), V((1024, 128), F32), V((1024, 128), F32),
-            V((16, 128), F32), V((16, 128), F32), V((128, 128), F32), V((128, 128), F32), V((128, 128), F32), V((128, 128), F32),
+            V((128, 128), F32), V((128, 128), F32), V((128, 128), F32), V((128, 128), F32), V((128, 128), F32), V((128, 128), F32),
             V((16, 128, 128), F32), V((16, 128, 128), F32),
             V((4, 1024, 128), BF16), V((8, SHARD, 128), BF16), V((8, SHARD, 128), BF16),
             V((128, 3 * SLOTS), F32), V((4, 128, 3 * SHARD), BF16), V((3 * SHARD, 256), BF16), V((128, 128), F32),
@@ -528,7 +530,7 @@
             V((2, 4, HALF, 128), BF16), V((2, 4, 8, 128), F32),
             V((4096, 1024), BF16), V((4, 2, 2, CHUNK, 1024), BF16),
             V((2, CHUNK, 1024), BF16), V((2, CHUNK, 1024), BF16), V((2, CHUNK, 1024), BF16),
-            DMA((14,)), DMA((4,)),
+            DMA((15,)), DMA((4,)),
             DMA((4,)), DMA((4,)),
             DMA((2, 8)), DMA((2, 8)),
             DMA((2, 4)), DMA((2, 4)),
@@ -545,7 +547,7 @@
         name="judge",
     )(
         queries, criteria_keys, criteria_values, candidate_keys, candidate_values,
-        jnp.asarray(cos), jnp.asarray(sin), out_weight, mine, hcos, hsin,
+        jnp.asarray(cos), jnp.asarray(sin), out_weight, lengths.reshape(1, 16), orders,
     )
 
 

time: 97.7 us -> 92.7 us (0.949)
  the two profiles are of different devices: /device:TPU:33 before, /device:TPU:42 now
where the time goes in v4:
time: 92.7 us; the launch traced here: 91.8 us
  Pallas kernels  90.1 us (97%)
  local copies, waits for them, and re-layouts  1.67 us (2%)
    pallas_call x1, Pallas kernels, local(): pl.pallas_call(fused_kernel, out_shape=jax.ShapeDtypeStruct((ROWS, 1024),...  90.1 us

profile of v4, /device:TPU:42, one launch (start us, length us, event | category | flops | bytes accessed | tf_op | source)
XLA Modules:
  0.0 91.8 jit_solution(2321733407939366859)
XLA Ops:
  0.0 90.1 %judge.1 = bf16[128,1024]{1,0:T(8,128)(2,1)} custom-call(bf16[128,1024]{1,0:T(8,128)(2,1)} %q_ref.1, bf16[128,128]{1,0:T(8,128)(2,1)} %rk_ref.1, bf16[128,128]{1,0:T(8,128)(2,1)} %rv_ref.1, bf16[512,128]{1,0:T(8,128)(2,1)} %ck_ref.1, bf16[512,128]{1,0:T(8,128)(2,1)} %cv_ref.1, f32[4480,128]{1,0:T(8,128)} %constant.4.clone.cos_ref, ...), custom_call_target="tpu_custom_call" | custom-call | tf_op jit(solution)/shard_map/judge/pallas_call | solution.py:515
  90.1 1.7 %copy.12 = bf16[128,1024]{1,0:T(8,128)(2,1)} copy(bf16[128,1024]{1,0:T(8,128)(2,1)} %judge.1) | data formatting | bytes 524288

commit v5 on v4

--- a/solution.py
+++ b/solution.py
@@ -273,13 +273,16 @@
     def unit_near(n, carry):
         slot = ordered(n, 0)
 
+        @pl.when(n == 1)
+        def _():
+            forward(1, 1)
+
         @pl.when(n == 2)
         def _():
-            forward(1, 1)
+            forward(1, 0)
 
         @pl.when(n == 3)
         def _():
-            forward(1, 0)
             arrived(qfwd)
 
         rotate(near, slot, one)
@@ -295,7 +298,7 @@
     def unit_second(n, carry):
         slot = lax.rem(y + n, 4)
 
-        @pl.when(n == 2)
+        @pl.when(n == 1)
         def _():
             forward(2, 0)
 

time: 92.7 us -> 92.9 us (level)
  no operation moved by 1% of the time
where the time goes in v5:
time: 92.9 us; the launch traced here: 92.6 us
  Pallas kernels  90.9 us (98%)
  local copies, waits for them, and re-layouts  1.67 us (2%)
    pallas_call x1, Pallas kernels, local(): pl.pallas_call(fused_kernel, out_shape=jax.ShapeDtypeStruct((ROWS, 1024),...  90.9 us

profile of v5, /device:TPU:42, one launch (start us, length us, event | category | flops | bytes accessed | tf_op | source)
XLA Modules:
  0.0 92.6 jit_solution(2770932864453624958)
XLA Ops:
  0.0 90.9 %judge.1 = bf16[128,1024]{1,0:T(8,128)(2,1)} custom-call(bf16[128,1024]{1,0:T(8,128)(2,1)} %q_ref.1, bf16[128,128]{1,0:T(8,128)(2,1)} %rk_ref.1, bf16[128,128]{1,0:T(8,128)(2,1)} %rv_ref.1, bf16[512,128]{1,0:T(8,128)(2,1)} %ck_ref.1, bf16[512,128]{1,0:T(8,128)(2,1)} %cv_ref.1, f32[4480,128]{1,0:T(8,128)} %constant.4.clone.cos_ref, ...), custom_call_target="tpu_custom_call" | custom-call | tf_op jit(solution)/shard_map/judge/pallas_call | solution.py:518
  90.9 1.7 %copy.12 = bf16[128,1024]{1,0:T(8,128)(2,1)} copy(bf16[128,1024]{1,0:T(8,128)(2,1)} %judge.1) | data formatting | bytes 524288
